TPU v7x, 32 devices: a whole 2x2x4 slice. The times are simulated.
32 devices in a mesh: groups: 2 (over x), ep: 4 (over z), et: 4 (over y, core).
Axes of the slice: x: 2, y: 2, z: 4, core: 2. Of those that a mesh axis runs over, the one named last changes fastest.
Arguments:
- hidden: bfloat16 [8, 768, 8192], P(('groups', 'ep'), None, 'et'), parts along dimension 0, may hold values from -1.75 to 1.75
- w_down: bfloat16 [4, 8192, 4096], P('ep', 'et'), may hold values from -0.09375 to 0.09375
- upstream: bfloat16 [2048, 4096], P(('groups', 'ep'), 'et'), parts along dimension 0, may hold values from -6 to 6
- expert_ids: int32 [2048, 2], P(('groups', 'ep')), parts along dimension 0, may hold values from 0 to 3, as said below
- combine: float32 [2048, 2], P(('groups', 'ep')), parts along dimension 0, may hold values from 0.09 to 1
Outputs:
- mixed: bfloat16 [2048, 4096], P(('groups', 'ep'), 'et'), parts along dimension 0
- grad_hidden: bfloat16 [8, 768, 8192], P(('groups', 'ep'), None, 'et'), parts along dimension 0
- grad_weight: bfloat16 [8, 8192, 4096], P(('groups', 'ep'), 'et'), parts along dimension 0
- balance: float32 [2], P('groups'), parts along dimension 0
There are 2 independent parts, one for each index of `groups`. A program takes and returns all parts, laid end to end along the dimension named above; an argument that names none is the same for every part. Nothing has to cross between parts.
Inputs may be any that keep to these rules, and one draw needn't show every extreme that they name: `expert_ids`: each token names 2 different experts; among the 256 tokens of one index of ep no expert is named more than 192 times, and some expert exactly 192 times; every expert is named by some token.
All inputs are finite; a program needn't handle non-finite values.
Results may differ from a plain program's by a relative error of at most 0.01.
Values may be sent and summed in bfloat16 or wider, within the bound.
A program may use at most 192 MiB of HBM per device.

v0:
```python
import jax
import jax.numpy as jnp
from jax import lax
from jax.sharding import PartitionSpec as P


def slot_numbers(expert_ids, experts_all):
    flat_ids = expert_ids.reshape(-1)
    onehot_table = (flat_ids[:, None] == jnp.arange(experts_all, dtype=jnp.int32)[None, :]).astype(
        jnp.int32
    )
    running = jnp.cumsum(onehot_table, axis=0, dtype=jnp.int32) - onehot_table
    slot_index = jnp.sum(running * onehot_table, axis=1)
    return (slot_index, onehot_table)


def on_device(hidden, w_down, upstream, expert_ids, combine):
    experts_all = lax.axis_size("ep")
    groups_et = lax.axis_size("et")
    tokens_here = upstream.shape[0]
    top_count = combine.shape[1]
    slot_rows = hidden.shape[1]
    capacity = slot_rows // experts_all
    model_width = w_down.shape[2]
    feature_cols = model_width // groups_et
    hidden_local = hidden[0]
    weight_local = w_down[0]
    slot_index, onehot_table = slot_numbers(expert_ids, experts_all)
    destination = expert_ids.reshape(-1) * capacity + slot_index
    columns = weight_local
    summed = lax.psum_scatter(
        lax.dot_general(
            columns, hidden_local, (((0,), (1,)), ((), ())), preferred_element_type=jnp.float32
        ).astype(jnp.bfloat16),
        "et",
        scatter_dimension=0,
        tiled=True,
    )
    returned = lax.all_to_all(summed, "ep", split_axis=1, concat_axis=1, tiled=True)
    picked = jnp.take(returned, destination, axis=1).astype(jnp.float32)
    picked = picked.reshape(feature_cols, tokens_here, top_count)
    mixed = jnp.sum(picked * combine[None, :, :], axis=2).T.astype(jnp.bfloat16)
    scaled = (combine[:, :, None] * upstream[:, None, :].astype(jnp.float32)).astype(jnp.bfloat16)
    buffer = jnp.zeros((experts_all * capacity, feature_cols), jnp.bfloat16)
    buffer = buffer.at[destination].set(scaled.reshape(-1, feature_cols))
    arrived = lax.all_to_all(buffer, "ep", split_axis=0, concat_axis=0, tiled=True)
    piece = lax.all_gather(arrived, "et", axis=1, tiled=True)
    columns = weight_local
    grad_h = lax.dot_general(
        piece, columns, (((1,), (1,)), ((), ())), preferred_element_type=jnp.float32
    )
    block_w = lax.dot_general(
        hidden_local, piece, (((0,), (0,)), ((), ())), preferred_element_type=jnp.float32
    )
    table_float = onehot_table.astype(jnp.float32)
    counts = jnp.sum(table_float, axis=0)
    masses = jnp.sum(table_float * combine.reshape(-1)[:, None], axis=0)
    counts_all, masses_all = lax.psum((counts, masses), "ep")
    tokens_all = tokens_here * experts_all
    balance = experts_all * jnp.sum(counts_all * masses_all) / (top_count * tokens_all * tokens_all)
    return (
        mixed,
        grad_h[None].astype(jnp.bfloat16),
        block_w[None].astype(jnp.bfloat16),
        jnp.reshape(balance, (1,)),
    )


def solution(mesh):
    placed = (
        P(("groups", "ep"), None, "et"),
        P("ep", "et", None),
        P(("groups", "ep"), "et"),
        P(("groups", "ep"), None),
        P(("groups", "ep"), None),
    )
    return jax.shard_map(
        on_device,
        mesh=mesh,
        in_specs=placed,
        out_specs=(
            P(("groups", "ep"), "et"),
            P(("groups", "ep"), None, "et"),
            P(("groups", "ep"), "et", None),
            P("groups"),
        ),
        check_vma=False,
    )
```

profile of v0, /device:TPU:0, one launch (start us, length us, event | category | flops | bytes accessed | tf_op | source)
XLA Modules:
  0.0 239.8 jit_solution(17536053356279079630)
XLA Ops:
  7.2 0.0 copy-start
  7.2 0.0 all-gather.2.cloned.1.call-start
  7.2 0.8 broadcast_multiply_fusion
  8.1 0.9 copy.20
  8.9 0.1 reshape.88
  9.1 0.1 eq.26
  9.2 0.1 copy.25
  9.4 0.1 mul.62
  9.5 0.8 copy.26
  10.3 0.1 mul.65
  10.5 1.2 reduce-window.6
  11.7 0.2 slice_reduce_fusion
  11.9 0.2 reduce-window.9
  12.1 0.1 add_bitcast_fusion
  12.2 2.9 %mul.67 = f32[256,2,1024]{2,1,0:T(2,128)} broadcast(bf16[256,1024]{1,0:T(8,128)(2,1)} %param.7), dimensions={0,2} | broadcast | bytes 2621440 | tf_op jit(solution)/shard_map/mul | solution.py:43
  15.1 3.6 %mul.68 = f32[512,1024]{1,0:T(8,128)} reshape(f32[256,2,1024]{2,1,0:T(2,128)} %mul.67) | data formatting | bytes 4194304 | tf_op jit(solution)/shard_map/mul | solution.py:43
  18.8 4.9 %scatter_custom_fusion = bf16[768,1024]{1,0:T(8,128)(2,1)} fusion(s32[512]{0:T(512)S(1)} %bitcast.54, f32[512,1024]{1,0:T(8,128)} %mul.68, f32[512]{0:T(512)S(1)} %mul.65, bf16[]{:T(256)} %constant.32.clone.1), kind=kCustom, calls=%fused_computation.15 | custom fusion | flops 1048576 | bytes 3672066 | tf_op jit(solution)/shard_map/scatter | solution.py:45
  23.7 43.4 %all_to_all.24 = bf16[4,192,1024]{2,1,0:T(8,128)(2,1)} all-to-all(bf16[4,192,1024]{2,1,0:T(8,128)(2,1)} %bitcast.50), channel_id=1, replica_groups=mesh['groups'=2,'ep'=4,'et'=4] {'ep'}, dimensions={0} | all-to-all | bytes 3145728 | tf_op jit(solution)/shard_map/all_to_all | solution.py:46
  67.1 0.0 all-gather.2.cloned.1.call-update
  67.1 0.2 reduce-scatter.2.cloned.1.call-start
  67.4 0.0 copy-done
  67.4 19.1 %fusion.4 = bf16[4096,768]{1,0:T(8,128)(2,1)} fusion(bf16[1,2048,4096]{2,1,0:T(8,128)(2,1)} %param.6, bf16[1,768,2048]{2,1,0:T(8,128)(2,1)S(1)} %copy-done), kind=kOutput, calls=%fused_computation.7 | convolution fusion | flops 12888047616 | bytes 26214400 | tf_op jit(solution)/shard_map/dot_general | solution.py:32
  86.5 0.0 copy-start.2
  86.5 0.0 reduce-scatter.2.cloned.1.call-update
  86.5 0.1 fusion.22
  86.7 9.8 %all-reduce = (f32[4]{0:T(128)S(1)}, f32[4]{0:T(128)S(1)}) all-reduce(f32[4]{0:T(128)S(1)} %get-tuple-element.17, f32[4]{0:T(128)S(1)} %get-tuple-element.16), channel_id=1, replica_groups=mesh['groups'=2,'ep'=4,'et'=4] {'ep'}, use_global_device_ids=true, to_apply=%region_7.8 | all-reduce | flops 8 | bytes 64 | tf_op jit(solution)/shard_map/psum | solution.py:58
  96.5 0.1 reduce_sum.50
  96.7 0.1 copy.22
  96.8 0.0 copy-done.2
  96.8 0.2 copy.23
  97.0 0.6 multiply_reduce_fusion.1
  98.2 14.6 %all-gather.2.cloned.1.call-done = bf16[768,4096]{1,0:T(8,128)(2,1)} async-done(((bf16[768,1024]{1,0:T(8,128)(2,1)}), bf16[768,4096]{1,0:T(8,128)(2,1)}) %all-gather.2.cloned.1.call-update) | async-done | bytes 6291472 | tf_op jit(solution)/shard_map/all_gather | solution.py:47
  112.8 18.8 %convert_bitcast_fusion = bf16[1,2048,4096]{1,2,0:T(8,128)(2,1)} fusion(bf16[768,4096]{1,0:T(8,128)(2,1)} %all-gather.2.cloned.1.call-done, bf16[1,768,2048]{2,1,0:T(8,128)(2,1)S(1)} %copy-done), kind=kOutput, calls=%fused_computation.6 | convolution fusion | flops 12893290496 | bytes 26214400 | tf_op jit(solution)/shard_map/dot_general | solution.py:52
  131.6 21.1 %copy.28 = bf16[1,2048,4096]{2,1,0:T(8,128)(2,1)} copy(bf16[1,2048,4096]{1,2,0:T(8,128)(2,1)} %convert_bitcast_fusion) | data formatting | bytes 33554432
  152.7 21.0 %reduce-scatter.2.cloned.1.call-done = bf16[1024,768]{1,0:T(8,128)(2,1)} async-done(((bf16[4096,768]{1,0:T(8,128)(2,1)}), bf16[1024,768]{1,0:T(8,128)(2,1)}) %reduce-scatter.2.cloned.1.call-update) | async-done | bytes 1572880 | tf_op jit(solution)/shard_map/reduce_scatter | solution.py:31
  173.7 2.6 %copy.24 = bf16[1024,768]{0,1:T(8,128)(2,1)} copy(bf16[1024,768]{1,0:T(8,128)(2,1)} %reduce-scatter.2.cloned.1.call-done) | data formatting | bytes 3145728 | tf_op jit(solution)/shard_map/reduce_scatter | solution.py:31
  176.3 4.6 %all-to-all-start = ((bf16[1024,4,192]{0,2,1:T(8,128)(2,1)}), bf16[1024,4,192]{0,2,1:T(8,128)(2,1)}, u32[]{:S(2)}, u32[]{:S(2)}) async-start(bf16[1024,4,192]{0,2,1:T(8,128)(2,1)} %bitcast.3), calls=%async_computation.1 | async-start | bytes 3145728 | tf_op jit(solution)/shard_map/all_to_all | solution.py:39
  180.9 19.7 %fusion.12 = bf16[1,768,2048]{2,1,0:T(8,128)(2,1)} fusion(bf16[768,4096]{1,0:T(8,128)(2,1)} %all-gather.2.cloned.1.call-done, bf16[1,2048,4096]{2,1,0:T(8,128)(2,1)} %param.6), kind=kOutput, calls=%fused_computation.11 | convolution fusion | flops 12886474752 | bytes 26214400 | tf_op jit(solution)/shard_map/dot_general | solution.py:49
  200.6 17.4 %all-to-all-done = bf16[1024,4,192]{0,2,1:T(8,128)(2,1)} async-done(((bf16[1024,4,192]{0,2,1:T(8,128)(2,1)}), bf16[1024,4,192]{0,2,1:T(8,128)(2,1)}, u32[]{:S(2)}, u32[]{:S(2)}) %all-to-all-start) | async-done | bytes 1572896 | tf_op jit(solution)/shard_map/all_to_all | solution.py:39
  218.0 0.0 copy-start.1
  218.0 5.2 %gather_fusion = bf16[512,1024]{1,0:T(8,128)(2,1)} fusion(bf16[1024,768]{0,1:T(8,128)(2,1)} %bitcast.4, s32[1024]{0:T(1024)S(1)} %pad_clamp_fusion), kind=kCustom, calls=%fused_computation | custom fusion | bytes 2099200 | tf_op jit(solution)/shard_map/jit(_take)/gather | solution.py:40
  223.2 2.3 gather.7
  225.5 6.3 %multiply_reduce_fusion = bf16[1024,256]{0,1:T(8,128)(2,1)} fusion(bf16[1024,256,2]{0,2,1:T(2,128)(2,1)} %gather.7, pred[256,2]{1,0:T(8,128)(4,1)S(1)} %copy.23, f32[256,2]{1,0:T(8,128)S(1)} %copy.26), kind=kLoop, calls=%fused_computation.13 | loop fusion | flops 1835008 | bytes 1575424 | tf_op jit(solution)/shard_map/reduce_sum | solution.py:42
  231.8 0.0 copy-done.1
  (5 shorter events, 0.1 us)
Async XLA Ops:
  7.2 60.2 %copy-start = (bf16[1,768,2048]{2,1,0:T(8,128)(2,1)S(1)}, bf16[1,768,2048]{2,1,0:T(8,128)(2,1)}, u32[]{:S(2)}) copy-start(bf16[1,768,2048]{2,1,0:T(8,128)(2,1)} %param.5) | copy-start | bytes 9437188
  7.2 105.6 %all-gather.2.cloned.1.call-start = ((), (), s32[]{:S(2)}) async-start(), calls=%async_computation.4 | async-start | bytes 7864320 | tf_op jit(solution)/shard_map/all_gather | solution.py:47
  67.1 106.6 %reduce-scatter.2.cloned.1.call-start = ((), (), s32[]{:S(2)}) async-start(), calls=%async_computation.3 | async-start | bytes 7864320 | tf_op jit(solution)/shard_map/reduce_scatter | solution.py:31
  86.5 10.2 %copy-start.2 = (s32[256,2]{0,1:T(2,128)S(1)}, s32[256,2]{0,1:T(2,128)}, u32[]{:S(2)}) copy-start(s32[256,2]{0,1:T(2,128)} %param.8) | copy-start | bytes 6148
  176.3 41.7 %all-to-all-start = ((bf16[1024,4,192]{0,2,1:T(8,128)(2,1)}), bf16[1024,4,192]{0,2,1:T(8,128)(2,1)}, u32[]{:S(2)}, u32[]{:S(2)}) async-start(bf16[1024,4,192]{0,2,1:T(8,128)(2,1)} %bitcast.3), calls=%async_computation.1 | async-start | bytes 3145728 | tf_op jit(solution)/shard_map/all_to_all | solution.py:39
  218.0 13.8 %copy-start.1 = (bf16[1,768,2048]{2,1,0:T(8,128)(2,1)S(1)}, bf16[1,768,2048]{2,1,0:T(8,128)(2,1)}, u32[]{:S(2)}) copy-start(bf16[1,768,2048]{2,1,0:T(8,128)(2,1)} %param.5) | copy-start | bytes 9437188
Sparse Core Ops, SparseCore 0:
  67.3 45.5 all-gather.1
  115.4 58.3 reduce-scatter.1
where the time goes:
time: 241 us; the launch traced here: 240 us
  matrix products  57.6 us (24%)
  blocking collectives  53.2 us (22%)
  waiting for transfers between devices  53 us (22%)
  local copies, waits for them, and re-layouts  40.7 us (17%)
  between operations  15.9 us (7%)
  other arithmetic  14.4 us (6%)
  starting transfers between devices  4.86 us (2%)
    all_to_all x1, blocking collectives, on_device(): lax.all_to_all(buffer, 'ep', split_axis=0, concat_axis=0, tiled=True)  43.4 us
    unnamed x9, local copies, waits for them, and re-layouts  22.8 us
    reduce_scatter x1, waiting for transfers between devices, on_device(): lax.psum_scatter(lax.dot_general(columns, hidden_local, (((0,), (1,)), ((...  21 us
    dot_general x1, matrix products, on_device(): lax.dot_general(piece, columns, (((1,), (1,)), ((), ())), preferred_eleme...  19.7 us
    dot_general x1, matrix products, on_device(): lax.dot_general(columns, hidden_local, (((0,), (1,)), ((), ())), preferre...  19.1 us
    dot_general x1, matrix products, on_device(): lax.dot_general(hidden_local, piece, (((0,), (0,)), ((), ())), preferred_...  18.8 us
    all_to_all x1, waiting for transfers between devices, on_device(): lax.all_to_all(summed, 'ep', split_axis=1, concat_axis=1, tiled=True)  17.4 us
    all_gather x1, waiting for transfers between devices, on_device(): piece = lax.all_gather(arrived, 'et', axis=1, tiled=True)  14.6 us
  transfers between devices with their start and end apart: 3, of which 3 were waited for; matrix products, arithmetic and copies ran while one was open for 33% of the time, Pallas kernels for 0%

commit v1 on v0

v1 whole, which is shorter than its diff:
```python
import functools

import jax
import jax.numpy as jnp
from jax import lax
from jax.experimental import pallas as pl
from jax.experimental.pallas import tpu as pltpu
from jax.sharding import PartitionSpec as P

F32 = jnp.float32
BF16 = jnp.bfloat16
VMEM_LIMIT = 40 * 1024 * 1024


def token_table(ids, combine, experts_all):
    tokens = ids.shape[0]
    columns = lax.broadcasted_iota(jnp.int32, (tokens, experts_all), 1)
    named = jnp.zeros((tokens, experts_all), F32)
    weight = jnp.zeros((tokens, experts_all), F32)
    for k in range(ids.shape[1]):
        hit = ids[:, k : k + 1] == columns
        named = named + jnp.where(hit, 1.0, 0.0)
        weight = weight + jnp.where(hit, combine[:, k : k + 1], 0.0)
    rows = lax.broadcasted_iota(jnp.int32, (tokens, tokens), 0)
    cols = lax.broadcasted_iota(jnp.int32, (tokens, tokens), 1)
    earlier = jnp.where(cols < rows, 1.0, 0.0).astype(BF16)
    slot = jnp.dot(earlier, named.astype(BF16), preferred_element_type=F32)
    return named, weight, slot


def pick_column(table, expert):
    columns = lax.broadcasted_iota(jnp.int32, table.shape, 1)
    return jnp.sum(jnp.where(columns == expert, table, 0.0), axis=1, keepdims=True)


def slot_matrix(named, slot, expert, capacity):
    hit = pick_column(named, expert) > 0.5
    place = pick_column(slot, expert).astype(jnp.int32)
    slots = lax.broadcasted_iota(jnp.int32, (named.shape[0], capacity), 1)
    return jnp.where((slots == place) & hit, 1.0, 0.0).astype(BF16)


def route_kernel(experts_all, capacity, me_ref, ids_ref, comb_ref, up_ref, *outs):
    me = me_ref[0]
    named, weight, slot = token_table(ids_ref[...], comb_ref[...], experts_all)
    upstream = up_ref[...].astype(F32)
    for s in range(experts_all):
        expert = lax.rem(me + s, experts_all)
        onehot = slot_matrix(named, slot, expert, capacity)
        scaled = (pick_column(weight, expert) * upstream).astype(BF16)
        outs[s][...] = lax.dot_general(
            onehot, scaled, (((0,), (0,)), ((), ())), preferred_element_type=F32
        ).astype(BF16)
    stats = outs[experts_all]
    stats[...] = jnp.zeros_like(stats)
    stats[0:1, 0:experts_all] = jnp.sum(named, axis=0, keepdims=True)
    stats[1:2, 0:experts_all] = jnp.sum(weight, axis=0, keepdims=True)


def route(me, ids, combine, upstream, experts_all, capacity):
    width = upstream.shape[1]
    vmem = pl.BlockSpec(memory_space=pltpu.VMEM)
    return pl.pallas_call(
        functools.partial(route_kernel, experts_all, capacity),
        out_shape=[jax.ShapeDtypeStruct((capacity, width), BF16)] * experts_all
        + [jax.ShapeDtypeStruct((8, 128), F32)],
        in_specs=[pl.BlockSpec(memory_space=pltpu.SMEM), vmem, vmem, vmem],
        out_specs=[vmem] * (experts_all + 1),
        compiler_params=pltpu.CompilerParams(vmem_limit_bytes=VMEM_LIMIT),
        name="route",
    )(me, ids, combine, upstream)


def mix_kernel(experts_all, capacity, me_ref, ids_ref, comb_ref, *refs):
    me = me_ref[0]
    out_ref = refs[experts_all]
    named, weight, slot = token_table(ids_ref[...], comb_ref[...], experts_all)
    total = None
    for s in range(experts_all):
        expert = lax.rem(me - s + experts_all, experts_all)
        onehot = slot_matrix(named, slot, expert, capacity)
        rows = jnp.dot(onehot, refs[s][...], preferred_element_type=F32)
        term = pick_column(weight, expert) * rows
        total = term if total is None else total + term
    out_ref[...] = total.astype(BF16)


def mix(me, ids, combine, returned, experts_all, capacity):
    width = returned[0].shape[1]
    vmem = pl.BlockSpec(memory_space=pltpu.VMEM)
    return pl.pallas_call(
        functools.partial(mix_kernel, experts_all, capacity),
        out_shape=jax.ShapeDtypeStruct((ids.shape[0], width), BF16),
        in_specs=[pl.BlockSpec(memory_space=pltpu.SMEM)] + [vmem] * (2 + experts_all),
        out_specs=vmem,
        compiler_params=pltpu.CompilerParams(vmem_limit_bytes=VMEM_LIMIT),
        name="mix",
    )(me, ids, combine, *returned)


def cost(rows, depth, columns):
    return pl.CostEstimate(
        flops=2 * rows * depth * columns,
        bytes_accessed=2 * (rows * depth + depth * columns + rows * columns),
        transcendentals=0,
    )


def tile_of(size, most):
    tile = min(size, most)
    while size % tile:
        tile //= 2
    return tile


def forward_kernel(j_ref, hidden_ref, w_ref, *refs):
    total = jnp.dot(hidden_ref[...], w_ref[...], preferred_element_type=F32)
    for extra in refs[:-1]:
        total = total + extra[...].astype(F32)
    refs[-1][...] = total.astype(BF16)


def forward_block(block, hidden, weight, width, extras=()):
    rows, depth = hidden.shape
    tile = tile_of(width, 256)
    tiles = width // tile
    out_spec = pl.BlockSpec((rows, tile), lambda i, j: (0, i))
    return pl.pallas_call(
        forward_kernel,
        out_shape=jax.ShapeDtypeStruct((rows, width), BF16),
        grid_spec=pltpu.PrefetchScalarGridSpec(
            num_scalar_prefetch=1,
            grid=(tiles,),
            in_specs=[
                pl.BlockSpec((rows, depth), lambda i, j: (0, 0)),
                pl.BlockSpec((depth, tile), lambda i, j: (0, j[0] * tiles + i)),
            ]
            + [out_spec] * len(extras),
            out_specs=out_spec,
        ),
        cost_estimate=cost(rows, depth, width),
        compiler_params=pltpu.CompilerParams(vmem_limit_bytes=VMEM_LIMIT),
        name="forward",
    )(block, hidden, weight, *extras)


def grad_h_kernel(blocks, width, j_ref, w_ref, *refs):
    total = None
    for q in range(blocks):
        start = pl.multiple_of(j_ref[q] * width, width)
        term = lax.dot_general(
            refs[q][...],
            w_ref[:, pl.ds(start, width)],
            (((1,), (1,)), ((), ())),
            preferred_element_type=F32,
        )
        total = term if total is None else total + term
    refs[blocks][...] = total.astype(BF16)


def grad_hidden_of(order, weight, pieces):
    depth, model = weight.shape
    rows, width = pieces[0].shape
    blocks = len(pieces)
    tile = tile_of(depth, 256)
    return pl.pallas_call(
        functools.partial(grad_h_kernel, blocks, width),
        out_shape=jax.ShapeDtypeStruct((rows, depth), BF16),
        grid_spec=pltpu.PrefetchScalarGridSpec(
            num_scalar_prefetch=1,
            grid=(depth // tile,),
            in_specs=[pl.BlockSpec((tile, model), lambda i, j: (i, 0))]
            + [pl.BlockSpec((rows, width), lambda i, j: (0, 0))] * blocks,
            out_specs=pl.BlockSpec((rows, tile), lambda i, j: (0, i)),
        ),
        cost_estimate=cost(rows, model, depth),
        compiler_params=pltpu.CompilerParams(vmem_limit_bytes=VMEM_LIMIT),
        name="grad_hidden",
    )(order, weight, *pieces)


def grad_w_kernel(has_base, j_ref, hidden_ref, piece_ref, *refs):
    refs[-1][...] = lax.dot_general(
        hidden_ref[...], piece_ref[...], (((0,), (0,)), ((), ())), preferred_element_type=F32
    ).astype(BF16)


def grad_weight_block(block, hidden, piece, model, base=None):
    rows, depth = hidden.shape
    width = piece.shape[1]
    tile = tile_of(depth, 512)
    extra = [] if base is None else [base]
    return pl.pallas_call(
        functools.partial(grad_w_kernel, bool(extra)),
        out_shape=jax.ShapeDtypeStruct((depth, model), BF16),
        grid_spec=pltpu.PrefetchScalarGridSpec(
            num_scalar_prefetch=1,
            grid=(depth // tile,),
            in_specs=[
                pl.BlockSpec((rows, tile), lambda i, j: (0, i)),
                pl.BlockSpec((rows, width), lambda i, j: (0, 0)),
            ]
            + [pl.BlockSpec(memory_space=pl.ANY)] * len(extra),
            out_specs=pl.BlockSpec((tile, width), lambda i, j: (i, j[0])),
        ),
        input_output_aliases={3: 0} if extra else {},
        cost_estimate=cost(depth, rows, width),
        compiler_params=pltpu.CompilerParams(vmem_limit_bytes=VMEM_LIMIT),
        name="grad_weight",
    )(block, hidden, piece, *extra)


def on_device(hidden, w_down, upstream, expert_ids, combine):
    experts_all = lax.axis_size("ep")
    et = lax.axis_size("et")
    chips = et // 2
    me = lax.axis_index("ep").astype(jnp.int32)
    here = lax.axis_index("et").astype(jnp.int32)
    tokens_here = upstream.shape[0]
    top_count = combine.shape[1]
    hidden_local = hidden[0]
    weight_local = w_down[0]
    capacity = hidden_local.shape[0] // experts_all
    model = weight_local.shape[1]
    width = model // et
    me_ref = me.reshape(1)

    def to_expert(x, s):
        return lax.ppermute(x, "ep", [(i, (i + s) % experts_all) for i in range(experts_all)])

    def to_core(x):
        return lax.ppermute(x, "et", [(i, i ^ 1) for i in range(et)])

    def to_chip(x, d):
        return lax.ppermute(x, "et", [(i, (i + 2 * d) % et) for i in range(et)])

    *routed, stats = route(me_ref, expert_ids, combine, upstream, experts_all, capacity)
    arrived = [routed[0]] + [to_expert(routed[s], s) for s in range(1, experts_all)]
    all_stats = [stats] + [to_expert(stats, s) for s in range(1, experts_all)]

    core_sums = []
    for d in list(range(1, chips)) + [0]:
        mine = lax.rem(here + 2 * d, et)
        other = mine + 1 - 2 * lax.rem(mine, 2)
        sent = to_core(forward_block(other.reshape(1), hidden_local, weight_local, width))
        block = forward_block(mine.reshape(1), hidden_local, weight_local, width, () if d else (sent,))
        if d:
            block = (block.astype(F32) + sent.astype(F32)).astype(BF16)
        core_sums.append(to_chip(block, d) if d else block)

    def result_rows(s):
        start = lax.rem(me + s, experts_all) * capacity
        parts = [lax.dynamic_slice_in_dim(x, start, capacity, 0).astype(F32) for x in core_sums]
        return functools.reduce(jnp.add, parts).astype(BF16)

    returned = [result_rows(0)] + [to_expert(result_rows(s), s) for s in range(1, experts_all)]
    mixed = mix(me_ref, expert_ids, combine, returned, experts_all, capacity)

    piece = jnp.zeros((experts_all * capacity, width), BF16)
    for s in range(experts_all):
        start = lax.rem(me - s + experts_all, experts_all) * capacity
        piece = lax.dynamic_update_slice_in_dim(piece, arrived[s], start, 0)
    pieces, order = [], []
    for d in range(chips):
        source = lax.rem(here - 2 * d + et, et)
        near = to_chip(piece, d) if d else piece
        pieces += [near, to_core(near)]
        order += [source, source + 1 - 2 * lax.rem(source, 2)]
    grad_w = None
    for block, near in zip(order, pieces):
        grad_w = grad_weight_block(block.reshape(1), hidden_local, near, model, grad_w)
    grad_h = grad_hidden_of(jnp.stack(order), weight_local, pieces)

    table = sum(
        jnp.where(
            (lax.rem(me - s + experts_all, experts_all) == jnp.arange(experts_all))[:, None, None],
            all_stats[s][None, :2, :experts_all],
            0.0,
        )
        for s in range(experts_all)
    )
    totals = jnp.sum(table, axis=0)
    tokens_all = tokens_here * experts_all
    balance = experts_all * jnp.sum(totals[0] * totals[1]) / (top_count * tokens_all * tokens_all)
    return (mixed, grad_h[None], grad_w[None], jnp.reshape(balance, (1,)))


def solution(mesh):
    placed = (
        P(("groups", "ep"), None, "et"),
        P("ep", "et", None),
        P(("groups", "ep"), "et"),
        P(("groups", "ep"), None),
        P(("groups", "ep"), None),
    )
    return jax.shard_map(
        on_device,
        mesh=mesh,
        in_specs=placed,
        out_specs=(
            P(("groups", "ep"), "et"),
            P(("groups", "ep"), None, "et"),
            P(("groups", "ep"), "et", None),
            P("groups"),
        ),
        check_vma=False,
    )
```

time: 241 us -> 157 us (0.65)
  the two profiles are of different devices: /device:TPU:0 before, /device:TPU:9 now
where the time goes in v1:
time: 157 us; the launch traced here: 156 us
  Pallas kernels  74.4 us (47%)
  waiting for transfers between devices  42.2 us (27%)
  starting transfers between devices  16.9 us (11%)
  local copies, waits for them, and re-layouts  13.9 us (9%)
  other arithmetic  6.1 us (4%)
  between operations  2.53 us (2%)
    pallas_call x4, Pallas kernels, grad_weight_block(): pl.pallas_call(functools.partial(grad_w_kernel, bool(extra)), out_shape=j...  26.6 us
    ppermute x9, waiting for transfers between devices, to_expert(): lax.ppermute(x, 'ep', [(i, (i + s) % experts_all) for i in range(experts_...  25.8 us
    pallas_call x4, Pallas kernels, forward_block(): pl.pallas_call(forward_kernel, out_shape=jax.ShapeDtypeStruct((rows, widt...  24.2 us
    pallas_call x1, Pallas kernels, grad_hidden_of(): pl.pallas_call(functools.partial(grad_h_kernel, blocks, width), out_shape...  19.5 us
    ppermute x2, waiting for transfers between devices, to_chip(): return lax.ppermute(x, 'et', [(i, (i + 2 * d) % et) for i in range(et)])  16.4 us
    ppermute x9, starting transfers between devices, to_expert(): lax.ppermute(x, 'ep', [(i, (i + s) % experts_all) for i in range(experts_...  11.3 us
    dynamic_update_slice x4, local copies, waits for them, and re-layouts, on_device(): piece = lax.dynamic_update_slice_in_dim(piece, arrived[s], start, 0)  7.26 us
    unnamed x10, local copies, waits for them, and re-layouts  5.31 us
  transfers between devices with their start and end apart: 15, of which 7 were waited for; matrix products, arithmetic and copies ran while one was open for 9% of the time, Pallas kernels for 45%

profile of v1, /device:TPU:9, one launch (start us, length us, event | category | flops | bytes accessed | tf_op | source)
XLA Modules:
  0.0 156.0 jit_solution(5801294435854017332)
XLA Ops:
  0.6 0.8 copy.16.ids_ref
  1.5 0.8 copy.17.comb_ref
  2.3 0.0 copy-start.2
  2.3 1.0 copy-done.2
  3.3 2.1 %route.1 = (bf16[192,1024]{1,0:T(8,128)(2,1)S(1)}, bf16[192,1024]{1,0:T(8,128)(2,1)}, bf16[192,1024]{1,0:T(8,128)(2,1)}, bf16[192,1024]{1,0:T(8,128)(2,1)}, f32[8,128]{1,0:T(8,128)S(1)}) custom-call(s32[1]{0:T(128)} %bitcast.me_ref, s32[256,2]{1,0:T(8,128)S(1)} %copy.16.ids_ref, f32[256,2]{1,0:T(8,128)S(1)} %copy.17.comb_ref, bf16[256,1024]{1,0:T(8,128)(2,1)S(1)} %copy-done.2), custom_call_target="tpu_custom_call" | custom-call | tf_op jit(solution)/shard_map/route/pallas_call | solution.py:63
  5.4 0.8 copy-done.3
  6.1 1.3 collective-permute-start.6
  7.4 1.0 collective-permute-start.7
  8.5 1.9 %copy-done = bf16[1,768,2048]{2,1,0:T(8,128)(2,1)S(1)} copy-done((bf16[1,768,2048]{2,1,0:T(8,128)(2,1)S(1)}, bf16[1,768,2048]{2,1,0:T(8,128)(2,1)}, u32[]{:S(2)}) %copy-start) | copy-done | bytes 3145752
  10.3 6.4 %forward.5 = bf16[768,1024]{1,0:T(8,128)(2,1)} custom-call(s32[1]{0:T(128)} %bitcast.4.j_ref, bf16[768,2048]{1,0:T(8,128)(2,1)S(1)} %bitcast.12, bf16[2048,4096]{1,0:T(8,128)(2,1)} %bitcast.21), custom_call_target="tpu_custom_call" | custom-call | flops 3221225472 | bytes 8912896 | tf_op jit(solution)/shard_map/forward/pallas_call | solution.py:128
  16.7 1.0 collective-permute-start
  17.7 1.7 %collective-permute-start.8 = (bf16[192,1024]{1,0:T(8,128)(2,1)}, bf16[192,1024]{1,0:T(8,128)(2,1)}, u32[]{:S(2)}, u32[]{:S(2)}) collective-permute-start(bf16[192,1024]{1,0:T(8,128)(2,1)} %get-tuple-element.12), channel_id=1, source_target_pairs={{0,12},{4,0},{8,4},{12,8},{1,13},{5,1},{9,5},{13,9},{2,14},{6,2},{... | collective-permute-start | bytes 1179656 | tf_op jit(solution)/shard_map/ppermute | solution.py:229
  19.4 1.3 broadcast_in_dim.70
  20.8 1.9 %constant_dynamic-update-slice_fusion.3 = bf16[768,1024]{1,0:T(8,128)(2,1)} fusion(bf16[768,1024]{1,0:T(8,128)(2,1)} %broadcast_in_dim.70, bf16[192,1024]{1,0:T(8,128)(2,1)} %copy-done.3, s32[]{:T(128)S(6)} %select_n.39), kind=kLoop, calls=%fused_computation.9 | loop fusion | bytes 786436 | tf_op jit(solution)/shard_map/dynamic_update_slice | solution.py:262
  22.7 1.8 %constant_dynamic-update-slice_fusion.2 = bf16[768,1024]{1,0:T(8,128)(2,1)} fusion(bf16[768,1024]{1,0:T(8,128)(2,1)} %constant_dynamic-update-slice_fusion.3, bf16[192,1024]{1,0:T(8,128)(2,1)} %collective-permute-done.6, s32[]{:T(128)S(6)} %select_n.38), kind=kLoop, calls=%fused_computation.8 | loop fusion | bytes 786436 | tf_op jit(solution)/shard_map/dynamic_update_slice | solution.py:262
  24.5 16.4 %collective-permute-done.7 = bf16[192,1024]{1,0:T(8,128)(2,1)} collective-permute-done((bf16[192,1024]{1,0:T(8,128)(2,1)}, bf16[192,1024]{1,0:T(8,128)(2,1)}, u32[]{:S(2)}, u32[]{:S(2)}) %collective-permute-start.7) | collective-permute-done | bytes 393248 | tf_op jit(solution)/shard_map/ppermute | solution.py:229
  40.8 1.8 %constant_dynamic-update-slice_fusion.1 = bf16[768,1024]{1,0:T(8,128)(2,1)} fusion(bf16[768,1024]{1,0:T(8,128)(2,1)} %constant_dynamic-update-slice_fusion.2, bf16[192,1024]{1,0:T(8,128)(2,1)} %collective-permute-done.7, s32[]{:T(128)S(6)} %select_n.37), kind=kLoop, calls=%fused_computation.7 | loop fusion | bytes 786436 | tf_op jit(solution)/shard_map/dynamic_update_slice | solution.py:262
  42.6 1.1 collective-permute-done.8
  43.7 1.8 %constant_dynamic-update-slice_fusion.refs_0_.piece_ref = bf16[768,1024]{1,0:T(8,128)(2,1)} fusion(bf16[768,1024]{1,0:T(8,128)(2,1)} %constant_dynamic-update-slice_fusion.1, bf16[192,1024]{1,0:T(8,128)(2,1)} %collective-permute-done.8, s32[]{:T(128)S(6)} %select_n.36), kind=kLoop, calls=%fused_computation.6 | loop fusion | bytes 786436 | tf_op jit(solution)/shard_map/dynamic_update_slice | solution.py:262
  45.4 1.2 collective-permute-start.10
  46.7 6.4 %forward.6 = bf16[768,1024]{1,0:T(8,128)(2,1)} custom-call(s32[1]{0:T(128)} %bitcast.6.j_ref, bf16[768,2048]{1,0:T(8,128)(2,1)S(1)} %bitcast.13, bf16[2048,4096]{1,0:T(8,128)(2,1)} %bitcast.22), custom_call_target="tpu_custom_call" | custom-call | flops 3221225472 | bytes 8912896 | tf_op jit(solution)/shard_map/forward/pallas_call | solution.py:128
  53.1 0.8 collective-permute-start.2
  53.9 0.1 collective-permute-start.9
  53.9 5.6 %forward.4 = bf16[768,1024]{1,0:T(8,128)(2,1)S(1)} custom-call(s32[1]{0:T(128)} %bitcast.1.j_ref, bf16[768,2048]{1,0:T(8,128)(2,1)S(1)} %bitcast.14, bf16[2048,4096]{1,0:T(8,128)(2,1)} %bitcast.23), custom_call_target="tpu_custom_call" | custom-call | flops 3221225472 | bytes 8912896 | tf_op jit(solution)/shard_map/forward/pallas_call | solution.py:128
  59.5 3.1 %collective-permute-start.13 = (f32[8,128]{1,0:T(8,128)S(1)}, f32[8,128]{1,0:T(8,128)S(1)}, u32[]{:S(2)}, u32[]{:S(2)}) collective-permute-start(f32[8,128]{1,0:T(8,128)S(1)} %get-tuple-element.13), channel_id=1, source_target_pairs={{0,8},{4,12},{8,0},{12,4},{1,9},{5,13},{9,1},{13,5},{2,10},{6,14},... | collective-permute-start | bytes 12296 | tf_op jit(solution)/shard_map/ppermute | solution.py:229
  62.7 3.3 %add_convert_fusion = bf16[768,1024]{1,0:T(8,128)(2,1)} fusion(bf16[768,1024]{1,0:T(8,128)(2,1)} %collective-permute-done, bf16[768,1024]{1,0:T(8,128)(2,1)S(1)} %forward.4), kind=kLoop, calls=%fused_computation | loop fusion | flops 3145728 | bytes 4718592 | tf_op jit(solution)/shard_map/convert_element_type | solution.py:248
  65.9 0.2 collective-permute-start.1
  66.2 1.7 %collective-permute-start.14 = (f32[8,128]{1,0:T(8,128)S(1)}, f32[8,128]{1,0:T(8,128)S(1)}, u32[]{:S(2)}, u32[]{:S(2)}) collective-permute-start(f32[8,128]{1,0:T(8,128)S(1)} %get-tuple-element.13), channel_id=1, source_target_pairs={{0,12},{4,0},{8,4},{12,8},{1,13},{5,1},{9,5},{13,9},{2,14},{6,2},{... | collective-permute-start | bytes 12296 | tf_op jit(solution)/shard_map/ppermute | solution.py:229
  67.9 0.1 pad_add_fusion.j_ref
  68.0 1.1 collective-permute-done.14
  69.1 12.1 %collective-permute-done.10.refs_2_.piece_ref = bf16[768,1024]{1,0:T(8,128)(2,1)} collective-permute-done((bf16[768,1024]{1,0:T(8,128)(2,1)}, bf16[768,1024]{1,0:T(8,128)(2,1)}, u32[]{:S(2)}, u32[]{:S(2)}) %collective-permute-start.10) | collective-permute-done | bytes 1572896 | tf_op jit(solution)/shard_map/ppermute | solution.py:235
  81.2 2.3 %collective-permute-start.11 = (bf16[768,1024]{1,0:T(8,128)(2,1)}, bf16[768,1024]{1,0:T(8,128)(2,1)}, u32[]{:S(2)}, u32[]{:S(2)}) collective-permute-start(bf16[768,1024]{1,0:T(8,128)(2,1)} %collective-permute-done.10.refs_2_.piece_ref), channel_id=1, source_target_pairs={{0,1},{1,0},{2,3},{3,2},{4,5},{5,4},{6,7},{7,6},{8,9},{9,8},{10,11... | collective-permute-start | bytes 4718600 | tf_op jit(solution)/shard_map/ppermute | solution.py:232
  83.5 0.1 add_reduce_fusion
  83.6 0.6 multiply_reduce_fusion
  84.9 6.7 %grad_weight.4.refs_0_ = bf16[2048,4096]{1,0:T(8,128)(2,1)} custom-call(s32[1]{0:T(128)} %bitcast.7.j_ref, bf16[768,2048]{1,0:T(8,128)(2,1)S(1)} %bitcast.15, bf16[768,1024]{1,0:T(8,128)(2,1)} %constant_dynamic-update-slice_fusion.refs_0_.piece_ref), custom_call_target="tpu_custom_call" | custom-call | flops 3221225472 | bytes 8912896 | tf_op jit(solution)/shard_map/grad_weight/pallas_call | solution.py:193
  91.5 5.8 %forward.7 = bf16[768,1024]{1,0:T(8,128)(2,1)S(1)} custom-call(s32[1]{0:T(128)} %bitcast.5.j_ref, bf16[768,2048]{1,0:T(8,128)(2,1)S(1)} %bitcast.16, bf16[2048,4096]{1,0:T(8,128)(2,1)} %bitcast.24, bf16[768,1024]{1,0:T(8,128)(2,1)} %collective-permute-done.2.refs_0_), custom_call_target="tpu_custom_call" | custom-call | flops 3221225472 | bytes 8912896 | tf_op jit(solution)/shard_map/forward/pallas_call | solution.py:128
  97.4 6.7 %grad_weight.5.refs_0_ = bf16[2048,4096]{1,0:T(8,128)(2,1)} custom-call(s32[1]{0:T(128)} %bitcast.8.j_ref, bf16[768,2048]{1,0:T(8,128)(2,1)S(1)} %bitcast.17, bf16[768,1024]{1,0:T(8,128)(2,1)} %collective-permute-done.9.refs_1_.piece_ref, bf16[2048,4096]{1,0:T(8,128)(2,1)} %grad_weight.4.refs_0_), custom_call_target="tpu_custom_call", output_to_operand_aliasing={{}: (3, {})} | custom-call | flops 3221225472 | bytes 8912896 | tf_op jit(solution)/shard_map/grad_weight/pallas_call | solution.py:193
  104.0 6.7 %grad_weight.6.refs_0_ = bf16[2048,4096]{1,0:T(8,128)(2,1)} custom-call(s32[1]{0:T(128)} %bitcast.1.j_ref, bf16[768,2048]{1,0:T(8,128)(2,1)S(1)} %bitcast.18, bf16[768,1024]{1,0:T(8,128)(2,1)} %collective-permute-done.10.refs_2_.piece_ref, bf16[2048,4096]{1,0:T(8,128)(2,1)} %grad_weight.5.refs_0_), custom_call_target="tpu_custom_call", output_to_operand_aliasing={{}: (3, {})} | custom-call | flops 3221225472 | bytes 8912896 | tf_op jit(solution)/shard_map/grad_weight/pallas_call | solution.py:193
  110.7 4.2 %collective-permute-done.1 = bf16[768,1024]{1,0:T(8,128)(2,1)} collective-permute-done((bf16[768,1024]{1,0:T(8,128)(2,1)}, bf16[768,1024]{1,0:T(8,128)(2,1)}, u32[]{:S(2)}, u32[]{:S(2)}) %collective-permute-start.1) | collective-permute-done | bytes 1572896 | tf_op jit(solution)/shard_map/ppermute | solution.py:235
  114.9 2.0 %add_convert_fusion.1 = (bf16[192,1024]{1,0:T(8,128)(2,1)S(1)}, bf16[192,1024]{1,0:T(8,128)(2,1)S(1)}, bf16[192,1024]{1,0:T(8,128)(2,1)S(1)}, bf16[192,1024]{1,0:T(8,128)(2,1)S(1)}) fusion(bf16[768,1024]{1,0:T(8,128)(2,1)S(1)} %forward.7, s32[]{:T(128)S(6)} %select_n.38, bf16[768,1024]{1,0:T(8,128)(2,1)} %collective-permute-done.1, s32[]{:T(128)S(6)} %select_n.37, ...), kind=kLoop, calls=%fused_computation.1 | loop fusion | flops 3145728 | bytes 4718608 | tf_op jit(solution)/shard_map/convert_element_type | solution.py:254
  117.0 0.1 collective-permute-start.3
  117.1 0.9 collective-permute-start.4
  118.0 1.4 collective-permute-start.5
  119.4 19.5 %grad_hidden.1 = bf16[768,2048]{1,0:T(8,128)(2,1)} custom-call(s32[4]{0:T(128)S(1)} %pad_add_fusion.j_ref, bf16[2048,4096]{1,0:T(8,128)(2,1)} %bitcast.25, bf16[768,1024]{1,0:T(8,128)(2,1)} %constant_dynamic-update-slice_fusion.refs_0_.piece_ref, bf16[768,1024]{1,0:T(8,128)(2,1)} %collective-permute-done.9.refs_1_.piece_ref, ...), custom_call_target="tpu_custom_call" | custom-call | flops 12884901888 | bytes 26214400 | tf_op jit(solution)/shard_map/grad_hidden/pallas_call | solution.py:166
  138.9 6.6 %grad_weight.7 = bf16[2048,4096]{1,0:T(8,128)(2,1)} custom-call(s32[1]{0:T(128)} %bitcast.4.j_ref, bf16[768,2048]{1,0:T(8,128)(2,1)S(1)} %bitcast.19, bf16[768,1024]{1,0:T(8,128)(2,1)} %collective-permute-done.11.refs_3_.piece_ref, bf16[2048,4096]{1,0:T(8,128)(2,1)} %grad_weight.6.refs_0_), custom_call_target="tpu_custom_call", output_to_operand_aliasing={{}: (3, {})} | custom-call | flops 3221225472 | bytes 8912896 | tf_op jit(solution)/shard_map/grad_weight/pallas_call | solution.py:193
  145.6 4.1 %collective-permute-done.4.refs_2_ = bf16[192,1024]{1,0:T(8,128)(2,1)S(1)} collective-permute-done((bf16[192,1024]{1,0:T(8,128)(2,1)S(1)}, bf16[192,1024]{1,0:T(8,128)(2,1)S(1)}, u32[]{:S(2)}, u32[]{:S(2)}) %collective-permute-start.4) | collective-permute-done | bytes 393248 | tf_op jit(solution)/shard_map/ppermute | solution.py:229
  149.7 3.1 %collective-permute-done.5.refs_3_ = bf16[192,1024]{1,0:T(8,128)(2,1)S(1)} collective-permute-done((bf16[192,1024]{1,0:T(8,128)(2,1)S(1)}, bf16[192,1024]{1,0:T(8,128)(2,1)S(1)}, u32[]{:S(2)}, u32[]{:S(2)}) %collective-permute-start.5) | collective-permute-done | bytes 393248 | tf_op jit(solution)/shard_map/ppermute | solution.py:229
  152.8 2.0 %mix.1 = bf16[256,1024]{1,0:T(8,128)(2,1)} custom-call(s32[1]{0:T(128)} %bitcast.me_ref, s32[256,2]{1,0:T(8,128)S(1)} %copy.16.ids_ref, f32[256,2]{1,0:T(8,128)S(1)} %copy.17.comb_ref, bf16[192,1024]{1,0:T(8,128)(2,1)S(1)} %get-tuple-element.17.refs_0_, bf16[192,1024]{1,0:T(8,128)(2,1)S(1)} %collective-permute-done.3.refs_1_, ...), custom_call_target="tpu_custom_call" | custom-call | tf_op jit(solution)/shard_map/mix/pallas_call | solution.py:91
  (19 shorter events, 0.0 us)
Async XLA Ops:
  2.3 1.0 copy-start.2
  5.4 0.8 copy-start.3
  6.1 16.5 %collective-permute-start.6 = (bf16[192,1024]{1,0:T(8,128)(2,1)}, bf16[192,1024]{1,0:T(8,128)(2,1)}, u32[]{:S(2)}, u32[]{:S(2)}) collective-permute-start(bf16[192,1024]{1,0:T(8,128)(2,1)} %get-tuple-element.10), channel_id=1, source_target_pairs={{0,4},{4,8},{8,12},{12,0},{1,5},{5,9},{9,13},{13,1},{2,6},{6,10},{... | collective-permute-start | bytes 1179656 | tf_op jit(solution)/shard_map/ppermute | solution.py:229
  7.4 33.4 %collective-permute-start.7 = (bf16[192,1024]{1,0:T(8,128)(2,1)}, bf16[192,1024]{1,0:T(8,128)(2,1)}, u32[]{:S(2)}, u32[]{:S(2)}) collective-permute-start(bf16[192,1024]{1,0:T(8,128)(2,1)} %get-tuple-element.11), channel_id=1, source_target_pairs={{0,8},{4,12},{8,0},{12,4},{1,9},{5,13},{9,1},{13,5},{2,10},{6,14},... | collective-permute-start | bytes 1179656 | tf_op jit(solution)/shard_map/ppermute | solution.py:229
  8.5 1.9 %copy-start = (bf16[1,768,2048]{2,1,0:T(8,128)(2,1)S(1)}, bf16[1,768,2048]{2,1,0:T(8,128)(2,1)}, u32[]{:S(2)}) copy-start(bf16[1,768,2048]{2,1,0:T(8,128)(2,1)} %param.5) | copy-start | bytes 9437188
  16.7 42.8 %collective-permute-start = (bf16[768,1024]{1,0:T(8,128)(2,1)}, bf16[768,1024]{1,0:T(8,128)(2,1)}, u32[]{:S(2)}, u32[]{:S(2)}) collective-permute-start(bf16[768,1024]{1,0:T(8,128)(2,1)} %forward.5), channel_id=1, source_target_pairs={{0,1},{1,0},{2,3},{3,2},{4,5},{5,4},{6,7},{7,6},{8,9},{9,8},{10,11... | collective-permute-start | bytes 4718600 | tf_op jit(solution)/shard_map/ppermute | solution.py:232
  17.7 26.0 %collective-permute-start.8 = (bf16[192,1024]{1,0:T(8,128)(2,1)}, bf16[192,1024]{1,0:T(8,128)(2,1)}, u32[]{:S(2)}, u32[]{:S(2)}) collective-permute-start(bf16[192,1024]{1,0:T(8,128)(2,1)} %get-tuple-element.12), channel_id=1, source_target_pairs={{0,12},{4,0},{8,4},{12,8},{1,13},{5,1},{9,5},{13,9},{2,14},{6,2},{... | collective-permute-start | bytes 1179656 | tf_op jit(solution)/shard_map/ppermute | solution.py:229
  20.8 25.9 %copy-start.1 = (bf16[1,768,2048]{2,1,0:T(8,128)(2,1)S(1)}, bf16[1,768,2048]{2,1,0:T(8,128)(2,1)}, u32[]{:S(2)}) copy-start(bf16[1,768,2048]{2,1,0:T(8,128)(2,1)} %param.5) | copy-start | bytes 9437188
  45.4 35.8 %collective-permute-start.10 = (bf16[768,1024]{1,0:T(8,128)(2,1)}, bf16[768,1024]{1,0:T(8,128)(2,1)}, u32[]{:S(2)}, u32[]{:S(2)}) collective-permute-start(bf16[768,1024]{1,0:T(8,128)(2,1)} %constant_dynamic-update-slice_fusion.refs_0_.piece_ref), channel_id=1, source_target_pairs={{0,2},{1,3},{2,0},{3,1},{4,6},{5,7},{6,4},{7,5},{8,10},{9,11},{10,... | collective-permute-start | bytes 4718600 | tf_op jit(solution)/shard_map/ppermute | solution.py:235
  53.1 38.5 %collective-permute-start.2 = (bf16[768,1024]{1,0:T(8,128)(2,1)}, bf16[768,1024]{1,0:T(8,128)(2,1)}, u32[]{:S(2)}, u32[]{:S(2)}) collective-permute-start(bf16[768,1024]{1,0:T(8,128)(2,1)} %forward.6), channel_id=1, source_target_pairs={{0,1},{1,0},{2,3},{3,2},{4,5},{5,4},{6,7},{7,6},{8,9},{9,8},{10,11... | collective-permute-start | bytes 4718600 | tf_op jit(solution)/shard_map/ppermute | solution.py:232
  53.9 12.1 %collective-permute-start.12 = (f32[8,128]{1,0:T(8,128)S(1)}, f32[8,128]{1,0:T(8,128)S(1)}, u32[]{:S(2)}, u32[]{:S(2)}) collective-permute-start(f32[8,128]{1,0:T(8,128)S(1)} %get-tuple-element.13), channel_id=1, source_target_pairs={{0,4},{4,8},{8,12},{12,0},{1,5},{5,9},{9,13},{13,1},{2,6},{6,10},{... | collective-permute-start | bytes 12296 | tf_op jit(solution)/shard_map/ppermute | solution.py:229
  53.9 43.5 %collective-permute-start.9 = (bf16[768,1024]{1,0:T(8,128)(2,1)}, bf16[768,1024]{1,0:T(8,128)(2,1)}, u32[]{:S(2)}, u32[]{:S(2)}) collective-permute-start(bf16[768,1024]{1,0:T(8,128)(2,1)} %constant_dynamic-update-slice_fusion.refs_0_.piece_ref), channel_id=1, source_target_pairs={{0,1},{1,0},{2,3},{3,2},{4,5},{5,4},{6,7},{7,6},{8,9},{9,8},{10,11... | collective-permute-start | bytes 4718600 | tf_op jit(solution)/shard_map/ppermute | solution.py:232
  59.5 6.7 %collective-permute-start.13 = (f32[8,128]{1,0:T(8,128)S(1)}, f32[8,128]{1,0:T(8,128)S(1)}, u32[]{:S(2)}, u32[]{:S(2)}) collective-permute-start(f32[8,128]{1,0:T(8,128)S(1)} %get-tuple-element.13), channel_id=1, source_target_pairs={{0,8},{4,12},{8,0},{12,4},{1,9},{5,13},{9,1},{13,5},{2,10},{6,14},... | collective-permute-start | bytes 12296 | tf_op jit(solution)/shard_map/ppermute | solution.py:229
  65.9 49.0 %collective-permute-start.1 = (bf16[768,1024]{1,0:T(8,128)(2,1)}, bf16[768,1024]{1,0:T(8,128)(2,1)}, u32[]{:S(2)}, u32[]{:S(2)}) collective-permute-start(bf16[768,1024]{1,0:T(8,128)(2,1)} %add_convert_fusion), channel_id=1, source_target_pairs={{0,2},{1,3},{2,0},{3,1},{4,6},{5,7},{6,4},{7,5},{8,10},{9,11},{10,... | collective-permute-start | bytes 4718600 | tf_op jit(solution)/shard_map/ppermute | solution.py:235
  66.2 2.9 %collective-permute-start.14 = (f32[8,128]{1,0:T(8,128)S(1)}, f32[8,128]{1,0:T(8,128)S(1)}, u32[]{:S(2)}, u32[]{:S(2)}) collective-permute-start(f32[8,128]{1,0:T(8,128)S(1)} %get-tuple-element.13), channel_id=1, source_target_pairs={{0,12},{4,0},{8,4},{12,8},{1,13},{5,1},{9,5},{13,9},{2,14},{6,2},{... | collective-permute-start | bytes 12296 | tf_op jit(solution)/shard_map/ppermute | solution.py:229
  81.2 38.2 %collective-permute-start.11 = (bf16[768,1024]{1,0:T(8,128)(2,1)}, bf16[768,1024]{1,0:T(8,128)(2,1)}, u32[]{:S(2)}, u32[]{:S(2)}) collective-permute-start(bf16[768,1024]{1,0:T(8,128)(2,1)} %collective-permute-done.10.refs_2_.piece_ref), channel_id=1, source_target_pairs={{0,1},{1,0},{2,3},{3,2},{4,5},{5,4},{6,7},{7,6},{8,9},{9,8},{10,11... | collective-permute-start | bytes 4718600 | tf_op jit(solution)/shard_map/ppermute | solution.py:232
  117.0 28.6 %collective-permute-start.3 = (bf16[192,1024]{1,0:T(8,128)(2,1)S(1)}, bf16[192,1024]{1,0:T(8,128)(2,1)S(1)}, u32[]{:S(2)}, u32[]{:S(2)}) collective-permute-start(bf16[192,1024]{1,0:T(8,128)(2,1)S(1)} %get-tuple-element.16), channel_id=1, source_target_pairs={{0,4},{4,8},{8,12},{12,0},{1,5},{5,9},{9,13},{13,1},{2,6},{6,10},{... | collective-permute-start | bytes 1179656 | tf_op jit(solution)/shard_map/ppermute | solution.py:229
  117.1 32.6 %collective-permute-start.4 = (bf16[192,1024]{1,0:T(8,128)(2,1)S(1)}, bf16[192,1024]{1,0:T(8,128)(2,1)S(1)}, u32[]{:S(2)}, u32[]{:S(2)}) collective-permute-start(bf16[192,1024]{1,0:T(8,128)(2,1)S(1)} %get-tuple-element.15), channel_id=1, source_target_pairs={{0,8},{4,12},{8,0},{12,4},{1,9},{5,13},{9,1},{13,5},{2,10},{6,14},... | collective-permute-start | bytes 1179656 | tf_op jit(solution)/shard_map/ppermute | solution.py:229
  118.0 34.8 %collective-permute-start.5 = (bf16[192,1024]{1,0:T(8,128)(2,1)S(1)}, bf16[192,1024]{1,0:T(8,128)(2,1)S(1)}, u32[]{:S(2)}, u32[]{:S(2)}) collective-permute-start(bf16[192,1024]{1,0:T(8,128)(2,1)S(1)} %get-tuple-element.14), channel_id=1, source_target_pairs={{0,12},{4,0},{8,4},{12,8},{1,13},{5,1},{9,5},{13,9},{2,14},{6,2},{... | collective-permute-start | bytes 1179656 | tf_op jit(solution)/shard_map/ppermute | solution.py:229

commit v2 on v1

--- a/solution.py
+++ b/solution.py
@@ -9,7 +9,7 @@
 
 F32 = jnp.float32
 BF16 = jnp.bfloat16
-VMEM_LIMIT = 40 * 1024 * 1024
+VMEM_LIMIT = 50 * 1024 * 1024
 
 
 def token_table(ids, combine, experts_all):
@@ -113,20 +113,20 @@
     return tile
 
 
-def forward_kernel(j_ref, hidden_ref, w_ref, *refs):
+def forward_kernel(extras, j_ref, hidden_ref, w_ref, *refs):
     total = jnp.dot(hidden_ref[...], w_ref[...], preferred_element_type=F32)
-    for extra in refs[:-1]:
+    for extra in refs[:extras]:
         total = total + extra[...].astype(F32)
     refs[-1][...] = total.astype(BF16)
 
 
-def forward_block(block, hidden, weight, width, extras=()):
+def forward_block(block, hidden, weight, width, extras=(), after=()):
     rows, depth = hidden.shape
-    tile = tile_of(width, 256)
+    tile = tile_of(width, 512)
     tiles = width // tile
     out_spec = pl.BlockSpec((rows, tile), lambda i, j: (0, i))
     return pl.pallas_call(
-        forward_kernel,
+        functools.partial(forward_kernel, len(extras)),
         out_shape=jax.ShapeDtypeStruct((rows, width), BF16),
         grid_spec=pltpu.PrefetchScalarGridSpec(
             num_scalar_prefetch=1,
@@ -135,79 +135,145 @@
                 pl.BlockSpec((rows, depth), lambda i, j: (0, 0)),
                 pl.BlockSpec((depth, tile), lambda i, j: (0, j[0] * tiles + i)),
             ]
-            + [out_spec] * len(extras),
+            + [out_spec] * len(extras)
+            + [pl.BlockSpec(memory_space=pl.ANY)] * len(after),
             out_specs=out_spec,
         ),
         cost_estimate=cost(rows, depth, width),
         compiler_params=pltpu.CompilerParams(vmem_limit_bytes=VMEM_LIMIT),
         name="forward",
-    )(block, hidden, weight, *extras)
-
-
-def grad_h_kernel(blocks, width, j_ref, w_ref, *refs):
-    total = None
-    for q in range(blocks):
-        start = pl.multiple_of(j_ref[q] * width, width)
-        term = lax.dot_general(
-            refs[q][...],
-            w_ref[:, pl.ds(start, width)],
-            (((1,), (1,)), ((), ())),
-            preferred_element_type=F32,
-        )
-        total = term if total is None else total + term
-    refs[blocks][...] = total.astype(BF16)
-
-
-def grad_hidden_of(order, weight, pieces):
-    depth, model = weight.shape
-    rows, width = pieces[0].shape
-    blocks = len(pieces)
-    tile = tile_of(depth, 256)
-    return pl.pallas_call(
-        functools.partial(grad_h_kernel, blocks, width),
-        out_shape=jax.ShapeDtypeStruct((rows, depth), BF16),
+    )(block, hidden, weight, *extras, *after)
+
+
+def last_forward_kernel(extras, experts_all, capacity, j_ref, hidden_ref, w_ref, *refs):
+    outs, scratch = refs[extras + 1 : -1], refs[-1]
+    total = jnp.dot(hidden_ref[...], w_ref[...], preferred_element_type=F32)
+    for extra in refs[:extras]:
+        total = total + extra[...].astype(F32)
+    scratch[...] = total.astype(BF16)
+    for s in range(experts_all):
+        start = pl.multiple_of(lax.rem(j_ref[1] + s, experts_all) * capacity, capacity)
+        outs[s][...] = scratch[pl.ds(start, capacity), :]
+    outs[experts_all][...] = refs[extras][...]
+
+
+def last_forward_block(block, hidden, weight, width, extras, stats, experts_all):
+    rows, depth = hidden.shape
+    capacity = rows // experts_all
+    tile = tile_of(width, 512)
+    tiles = width // tile
+    stats_spec = pl.BlockSpec(stats.shape, lambda i, j: (0, 0))
+    return pl.pallas_call(
+        functools.partial(last_forward_kernel, len(extras), experts_all, capacity),
+        out_shape=[jax.ShapeDtypeStruct((capacity, width), BF16)] * experts_all
+        + [jax.ShapeDtypeStruct(stats.shape, stats.dtype)],
         grid_spec=pltpu.PrefetchScalarGridSpec(
             num_scalar_prefetch=1,
-            grid=(depth // tile,),
-            in_specs=[pl.BlockSpec((tile, model), lambda i, j: (i, 0))]
-            + [pl.BlockSpec((rows, width), lambda i, j: (0, 0))] * blocks,
-            out_specs=pl.BlockSpec((rows, tile), lambda i, j: (0, i)),
+            grid=(tiles,),
+            in_specs=[
+                pl.BlockSpec((rows, depth), lambda i, j: (0, 0)),
+                pl.BlockSpec((depth, tile), lambda i, j: (0, j[0] * tiles + i)),
+            ]
+            + [pl.BlockSpec((rows, tile), lambda i, j: (0, i))] * len(extras)
+            + [stats_spec],
+            out_specs=[pl.BlockSpec((capacity, tile), lambda i, j: (0, i))] * experts_all
+            + [stats_spec],
+            scratch_shapes=[pltpu.VMEM((rows, tile), BF16)],
         ),
-        cost_estimate=cost(rows, model, depth),
-        compiler_params=pltpu.CompilerParams(vmem_limit_bytes=VMEM_LIMIT),
-        name="grad_hidden",
-    )(order, weight, *pieces)
-
-
-def grad_w_kernel(has_base, j_ref, hidden_ref, piece_ref, *refs):
-    refs[-1][...] = lax.dot_general(
-        hidden_ref[...], piece_ref[...], (((0,), (0,)), ((), ())), preferred_element_type=F32
+        cost_estimate=cost(rows, depth, width),
+        compiler_params=pltpu.CompilerParams(vmem_limit_bytes=VMEM_LIMIT),
+        name="last_forward",
+    )(block, hidden, weight, *extras, stats)
+
+
+def add_kernel(a_ref, b_ref, out_ref):
+    out_ref[...] = (a_ref[...].astype(F32) + b_ref[...].astype(F32)).astype(BF16)
+
+
+def add(a, b):
+    rows, width = a.shape
+    spec = pl.BlockSpec((tile_of(rows, 256), width), lambda i: (i, 0))
+    return pl.pallas_call(
+        add_kernel,
+        out_shape=jax.ShapeDtypeStruct(a.shape, BF16),
+        grid=(rows // spec.block_shape[0],),
+        in_specs=[spec, spec],
+        out_specs=spec,
+        compiler_params=pltpu.CompilerParams(vmem_limit_bytes=VMEM_LIMIT),
+        name="add",
+    )(a, b)
+
+
+def grads_kernel(experts_all, first, last, tile, j_ref, hidden_ref, w_ref, *refs):
+    pieces, rest = refs[:4], refs[4:]
+    out_w, out_h, scratch = rest[-3:]
+    step = pl.program_id(0)
+    core, me = j_ref[1], j_ref[2]
+    capacity, width = pieces[0].shape
+
+    @pl.when(step == 0)
+    def _():
+        for half in range(2):
+            side = core if half == 0 else 1 - core
+            column = pl.multiple_of(side * width, width)
+            for s in range(experts_all):
+                owner = lax.rem(me - s + experts_all, experts_all)
+                row = pl.multiple_of(owner * capacity, capacity)
+                if s == 0:
+                    rows = pieces[2 * half][...]
+                else:
+                    rows = pieces[2 * half + 1][(s - 1) * capacity : s * capacity, :]
+                scratch[pl.ds(row, capacity), pl.ds(column, width)] = rows
+
+    columns = scratch[:, pl.ds(pl.multiple_of(step * tile, tile), tile)]
+    out_w[...] = lax.dot_general(
+        hidden_ref[...], columns, (((0,), (0,)), ((), ())), preferred_element_type=F32
     ).astype(BF16)
-
-
-def grad_weight_block(block, hidden, piece, model, base=None):
+    total = lax.dot_general(
+        scratch[...], w_ref[...], (((1,), (1,)), ((), ())), preferred_element_type=F32
+    )
+    if not first:
+        total = total + rest[0][...]
+    out_h[...] = total.astype(out_h.dtype)
+
+
+def grads(place, hidden, weight, pieces, experts_all, before, last):
     rows, depth = hidden.shape
-    width = piece.shape[1]
-    tile = tile_of(depth, 512)
-    extra = [] if base is None else [base]
-    return pl.pallas_call(
-        functools.partial(grad_w_kernel, bool(extra)),
-        out_shape=jax.ShapeDtypeStruct((depth, model), BF16),
+    model = weight.shape[1]
+    width = pieces[0].shape[1]
+    chip_width = 2 * width
+    steps = max(1, min(chip_width, depth) // 512)
+    tile_w, tile_h = chip_width // steps, depth // steps
+    whole = lambda x: pl.BlockSpec(x.shape, lambda i, j: (0, 0))
+    h_spec = pl.BlockSpec((rows, tile_h), lambda i, j: (0, i))
+    first = before is None
+    extra = [] if first else [before[1], before[0]]
+    return pl.pallas_call(
+        functools.partial(grads_kernel, experts_all, first, last, tile_w),
+        out_shape=[
+            jax.ShapeDtypeStruct((depth, model), BF16),
+            jax.ShapeDtypeStruct((rows, depth), BF16 if last else F32),
+        ],
         grid_spec=pltpu.PrefetchScalarGridSpec(
             num_scalar_prefetch=1,
-            grid=(depth // tile,),
+            grid=(steps,),
             in_specs=[
-                pl.BlockSpec((rows, tile), lambda i, j: (0, i)),
-                pl.BlockSpec((rows, width), lambda i, j: (0, 0)),
+                whole(hidden),
+                pl.BlockSpec((tile_h, chip_width), lambda i, j: (i, j[0])),
             ]
-            + [pl.BlockSpec(memory_space=pl.ANY)] * len(extra),
-            out_specs=pl.BlockSpec((tile, width), lambda i, j: (i, j[0])),
+            + [whole(x) for x in pieces]
+            + ([] if first else [h_spec, pl.BlockSpec(memory_space=pl.ANY)]),
+            out_specs=[
+                pl.BlockSpec((depth, tile_w), lambda i, j: (0, j[0] * steps + i)),
+                h_spec,
+            ],
+            scratch_shapes=[pltpu.VMEM((rows, chip_width), BF16)],
         ),
-        input_output_aliases={3: 0} if extra else {},
-        cost_estimate=cost(depth, rows, width),
-        compiler_params=pltpu.CompilerParams(vmem_limit_bytes=VMEM_LIMIT),
-        name="grad_weight",
-    )(block, hidden, piece, *extra)
+        input_output_aliases={} if first else {8: 0},
+        cost_estimate=cost(rows, depth, 2 * chip_width),
+        compiler_params=pltpu.CompilerParams(vmem_limit_bytes=VMEM_LIMIT),
+        name="grads",
+    )(place, hidden, weight, *pieces, *extra)
 
 
 def on_device(hidden, w_down, upstream, expert_ids, combine):
@@ -216,6 +282,7 @@
     chips = et // 2
     me = lax.axis_index("ep").astype(jnp.int32)
     here = lax.axis_index("et").astype(jnp.int32)
+    core = lax.rem(here, 2)
     tokens_here = upstream.shape[0]
     top_count = combine.shape[1]
     hidden_local = hidden[0]
@@ -235,41 +302,41 @@
         return lax.ppermute(x, "et", [(i, (i + 2 * d) % et) for i in range(et)])
 
     *routed, stats = route(me_ref, expert_ids, combine, upstream, experts_all, capacity)
-    arrived = [routed[0]] + [to_expert(routed[s], s) for s in range(1, experts_all)]
-    all_stats = [stats] + [to_expert(stats, s) for s in range(1, experts_all)]
-
-    core_sums = []
-    for d in list(range(1, chips)) + [0]:
+    own_rows = routed[0]
+    own_at = [to_chip(own_rows, d) if d else own_rows for d in range(chips)]
+    far_rows = jnp.concatenate([to_expert(routed[s], s) for s in range(1, experts_all)], axis=0)
+
+    arrived, after = [], ()
+    for d in range(1, chips):
         mine = lax.rem(here + 2 * d, et)
-        other = mine + 1 - 2 * lax.rem(mine, 2)
-        sent = to_core(forward_block(other.reshape(1), hidden_local, weight_local, width))
-        block = forward_block(mine.reshape(1), hidden_local, weight_local, width, () if d else (sent,))
-        if d:
-            block = (block.astype(F32) + sent.astype(F32)).astype(BF16)
-        core_sums.append(to_chip(block, d) if d else block)
-
-    def result_rows(s):
-        start = lax.rem(me + s, experts_all) * capacity
-        parts = [lax.dynamic_slice_in_dim(x, start, capacity, 0).astype(F32) for x in core_sums]
-        return functools.reduce(jnp.add, parts).astype(BF16)
-
-    returned = [result_rows(0)] + [to_expert(result_rows(s), s) for s in range(1, experts_all)]
+        other = mine + 1 - 2 * core
+        sent = forward_block(other.reshape(1), hidden_local, weight_local, width, (), after)
+        block = forward_block(mine.reshape(1), hidden_local, weight_local, width, (), (sent,))
+        after = (block,)
+        arrived.append(to_chip(add(block, to_core(sent)), d))
+    other = here + 1 - 2 * core
+    sent = to_core(forward_block(other.reshape(1), hidden_local, weight_local, width, (), after))
+
+    far_at = [to_chip(far_rows, d) if d else far_rows for d in range(chips)]
+    gradients = None
+    results = None
+    for d in range(chips):
+        chip = lax.rem(here // 2 - d + chips, chips)
+        pieces = [own_at[d], far_at[d], to_core(own_at[d]), to_core(far_at[d])]
+        place = jnp.stack([chip, core, me])
+        gradients = grads(
+            place, hidden_local, weight_local, pieces, experts_all, gradients, d == chips - 1
+        )
+        if d == 0:
+            results = last_forward_block(
+                jnp.stack([here, me]), hidden_local, weight_local, width, [sent, *arrived], stats, experts_all
+            )
+    grad_w, grad_h = gradients
+
+    *result, stats_late = results
+    returned = [result[0]] + [to_expert(result[s], s) for s in range(1, experts_all)]
+    all_stats = [stats_late] + [to_expert(stats_late, s) for s in range(1, experts_all)]
     mixed = mix(me_ref, expert_ids, combine, returned, experts_all, capacity)
-
-    piece = jnp.zeros((experts_all * capacity, width), BF16)
-    for s in range(experts_all):
-        start = lax.rem(me - s + experts_all, experts_all) * capacity
-        piece = lax.dynamic_update_slice_in_dim(piece, arrived[s], start, 0)
-    pieces, order = [], []
-    for d in range(chips):
-        source = lax.rem(here - 2 * d + et, et)
-        near = to_chip(piece, d) if d else piece
-        pieces += [near, to_core(near)]
-        order += [source, source + 1 - 2 * lax.rem(source, 2)]
-    grad_w = None
-    for block, near in zip(order, pieces):
-        grad_w = grad_weight_block(block.reshape(1), hidden_local, near, model, grad_w)
-    grad_h = grad_hidden_of(jnp.stack(order), weight_local, pieces)
 
     table = sum(
         jnp.where(

time: 157 us -> 173 us (1.10)
  waiting for transfers between devices: 42.2 us -> 76 us
  local copies, waits for them, and re-layouts: 13.9 us -> 3.35 us
  other arithmetic: 6.1 us -> 0.94 us
  Pallas kernels: 74.4 us -> 72.6 us
    ppermute x2 -> x3, waiting for transfers between devices: 16.4 us -> 49.2 us  [to_chip(): return lax.ppermute(x, 'et', [(i, (i + 2 * d) % et) for i in range(et)])]
    dynamic_update_slice x4 -> x0, local copies, waits for them, and re-layouts: 7.26 us -> none  [on_device(): piece = lax.dynamic_update_slice_in_dim(piece, arrived[s], start, 0)]
    convert_element_type x2 -> x0, other arithmetic: 5.32 us -> none  [the longest x1 3.28 us: on_device(): block = (block.astype(F32) + sent.astype(F32)).astype(BF16)]
    unnamed x10, local copies, waits for them, and re-layouts: 5.31 us -> 2.32 us
    pallas_call x9 -> x7, Pallas kernels: 70.3 us -> 68.5 us  [the longest x2 38.6 us: grads(): pl.pallas_call(functools.partial(grads_kernel, experts_all, first, last,...]
    ppermute x4 -> x6, starting transfers between devices: 4.07 us -> 3.64 us  [to_core(): return lax.ppermute(x, 'et', [(i, i ^ 1) for i in range(et)])]
  transfers between devices with their start and end apart: 15 -> 18, of which waited for: 7 -> 5; matrix products, arithmetic and copies ran while one was open for 9% -> 2% of each run, Pallas kernels for 45% -> 37%
where the time goes in v2:
time: 173 us; the launch traced here: 172 us
  waiting for transfers between devices  76 us (44%)
  Pallas kernels  72.6 us (42%)
  starting transfers between devices  16.7 us (10%)
  local copies, waits for them, and re-layouts  3.35 us (2%)
  between operations  2.63 us (2%)
    ppermute x3, waiting for transfers between devices, to_chip(): return lax.ppermute(x, 'et', [(i, (i + 2 * d) % et) for i in range(et)])  49.2 us
    pallas_call x2, Pallas kernels, grads(): pl.pallas_call(functools.partial(grads_kernel, experts_all, first, last,...  38.6 us
    ppermute x9, waiting for transfers between devices, to_expert(): lax.ppermute(x, 'ep', [(i, (i + s) % experts_all) for i in range(experts_...  26.8 us
    pallas_call x3, Pallas kernels, forward_block(): pl.pallas_call(functools.partial(forward_kernel, len(extras)), out_shape=...  19.6 us
    ppermute x9, starting transfers between devices, to_expert(): lax.ppermute(x, 'ep', [(i, (i + s) % experts_all) for i in range(experts_...  10.2 us
    pallas_call x1, Pallas kernels, last_forward_block(): pl.pallas_call(functools.partial(last_forward_kernel, len(extras), expert...  7.94 us
    ppermute x6, starting transfers between devices, to_core(): return lax.ppermute(x, 'et', [(i, i ^ 1) for i in range(et)])  3.64 us
  transfers between devices with their start and end apart: 18, of which 5 were waited for; matrix products, arithmetic and copies ran while one was open for 2% of the time, Pallas kernels for 37%

profile of v2, /device:TPU:9, one launch (start us, length us, event | category | flops | bytes accessed | tf_op | source)
XLA Modules:
  0.0 172.2 jit_solution(11162983418122890797)
XLA Ops:
  0.7 6.3 %forward.3.refs_0_ = bf16[768,1024]{1,0:T(8,128)(2,1)S(1)} custom-call(s32[1]{0:T(128)} %bitcast.6.j_ref, bf16[768,2048]{1,0:T(8,128)(2,1)} %bitcast.19, bf16[2048,4096]{1,0:T(8,128)(2,1)} %bitcast.13), custom_call_target="tpu_custom_call" | custom-call | flops 3221225472 | bytes 8912896 | tf_op jit(solution)/shard_map/forward/pallas_call | solution.py:128
  7.0 0.7 collective-permute-start.1
  7.7 0.1 copy.16.ids_ref
  7.9 0.1 copy.17.comb_ref
  8.0 2.1 %route.1 = (bf16[192,1024]{1,0:T(8,128)(2,1)}, bf16[192,1024]{1,0:T(8,128)(2,1)}, bf16[192,1024]{1,0:T(8,128)(2,1)}, bf16[192,1024]{1,0:T(8,128)(2,1)}, f32[8,128]{1,0:T(8,128)S(1)}) custom-call(s32[1]{0:T(128)} %bitcast.me_ref, s32[256,2]{1,0:T(8,128)S(1)} %copy.16.ids_ref, f32[256,2]{1,0:T(8,128)S(1)} %copy.17.comb_ref, bf16[256,1024]{1,0:T(8,128)(2,1)S(1)} %copy-done), custom_call_target="tpu_custom_call" | custom-call | tf_op jit(solution)/shard_map/route/pallas_call | solution.py:63
  10.1 1.3 collective-permute-start.7
  11.4 1.0 collective-permute-start.8
  12.4 1.5 collective-permute-start.9
  13.9 6.2 %forward.4.refs_0_.a_ref = bf16[768,1024]{1,0:T(8,128)(2,1)S(1)} custom-call(s32[1]{0:T(128)} %bitcast.5.j_ref, bf16[768,2048]{1,0:T(8,128)(2,1)} %bitcast.20, bf16[2048,4096]{1,0:T(8,128)(2,1)} %bitcast.14, bf16[768,1024]{1,0:T(8,128)(2,1)S(1)} %forward.3.refs_0_), custom_call_target="tpu_custom_call" | custom-call | flops 3221225472 | bytes 8912896 | tf_op jit(solution)/shard_map/forward/pallas_call | solution.py:128
  20.1 7.0 %forward.5 = bf16[768,1024]{1,0:T(8,128)(2,1)} custom-call(s32[1]{0:T(128)} %bitcast.4.j_ref, bf16[768,2048]{1,0:T(8,128)(2,1)} %bitcast.21, bf16[2048,4096]{1,0:T(8,128)(2,1)} %bitcast.15, bf16[768,1024]{1,0:T(8,128)(2,1)S(1)} %forward.4.refs_0_.a_ref), custom_call_target="tpu_custom_call" | custom-call | flops 3221225472 | bytes 8912896 | tf_op jit(solution)/shard_map/forward/pallas_call | solution.py:128
  27.2 0.9 collective-permute-start
  28.0 2.4 %add.75 = bf16[768,1024]{1,0:T(8,128)(2,1)S(1)} custom-call(bf16[768,1024]{1,0:T(8,128)(2,1)S(1)} %forward.4.refs_0_.a_ref, bf16[768,1024]{1,0:T(8,128)(2,1)} %collective-permute-done.1.b_ref), custom_call_target="tpu_custom_call" | custom-call | tf_op jit(solution)/shard_map/add/pallas_call | solution.py:196
  30.4 1.3 collective-permute-start.2
  31.7 0.0 collective-permute-done.7
  31.7 1.0 constant_dynamic-update-slice_fusion.2
  32.8 12.8 %collective-permute-done.8 = bf16[192,1024]{1,0:T(8,128)(2,1)} collective-permute-done((bf16[192,1024]{1,0:T(8,128)(2,1)}, bf16[192,1024]{1,0:T(8,128)(2,1)}, u32[]{:S(2)}, u32[]{:S(2)}) %collective-permute-start.8) | collective-permute-done | bytes 393248 | tf_op jit(solution)/shard_map/ppermute | solution.py:296
  45.5 1.0 constant_dynamic-update-slice_fusion.1
  46.5 1.1 collective-permute-done.9
  47.7 1.0 constant_dynamic-update-slice_fusion.refs_1_
  48.7 1.3 collective-permute-start.10
  50.0 0.7 collective-permute-start.14
  50.7 0.2 collective-permute-start.6
  51.0 0.1 add_add_fusion.1.j_ref
  51.0 0.1 add_add_fusion.j_ref
  51.1 49.2 %collective-permute-done.6.refs_0_ = bf16[192,1024]{1,0:T(8,128)(2,1)} collective-permute-done((bf16[192,1024]{1,0:T(8,128)(2,1)}, bf16[192,1024]{1,0:T(8,128)(2,1)}, u32[]{:S(2)}, u32[]{:S(2)}) %collective-permute-start.6) | collective-permute-done | bytes 393248 | tf_op jit(solution)/shard_map/ppermute | solution.py:302
  100.3 0.8 collective-permute-start.13
  101.1 0.1 pad_add_fusion.j_ref
  101.2 0.0 collective-permute-done.10.refs_1_
  101.2 0.0 collective-permute-start.11
  101.2 0.0 collective-permute-done.refs_0_
  101.2 0.5 collective-permute-start.12
  101.7 0.0 collective-permute-done.2.refs_1_
  101.7 7.9 %last_forward.1 = (bf16[192,1024]{1,0:T(8,128)(2,1)S(1)}, bf16[192,1024]{1,0:T(8,128)(2,1)S(1)}, bf16[192,1024]{1,0:T(8,128)(2,1)S(1)}, bf16[192,1024]{1,0:T(8,128)(2,1)S(1)}, f32[8,128]{1,0:T(8,128)S(1)}) custom-call(s32[2]{0:T(128)S(1)} %pad_add_fusion.j_ref, bf16[768,2048]{1,0:T(8,128)(2,1)} %bitcast.22, bf16[2048,4096]{1,0:T(8,128)(2,1)} %bitcast.16, ...), custom_call_target="tpu_custom_call" | custom-call | flops 3221225472 | bytes 8912896 | tf_op jit(solution)/shard_map/last_forward/pallas_call | solution.py:166
  109.6 0.1 collective-permute-start.15
  109.7 0.0 collective-permute-done.13.refs_2_
  109.7 19.3 %grads.2 = (bf16[2048,4096]{1,0:T(8,128)(2,1)}, f32[768,2048]{1,0:T(8,128)}) custom-call(s32[3]{0:T(128)S(1)} %add_add_fusion.1.j_ref, bf16[768,2048]{1,0:T(8,128)(2,1)} %bitcast.23, bf16[2048,4096]{1,0:T(8,128)(2,1)} %bitcast.17, bf16[192,1024]{1,0:T(8,128)(2,1)} %get-tuple-element.23.refs_0_, ...), custom_call_target="tpu_custom_call" | custom-call | flops 12884901888 | bytes 26214400 | tf_op jit(solution)/shard_map/grads/pallas_call | solution.py:251
  129.0 3.1 %collective-permute-start.16 = (f32[8,128]{1,0:T(8,128)S(1)}, f32[8,128]{1,0:T(8,128)S(1)}, u32[]{:S(2)}, u32[]{:S(2)}) collective-permute-start(f32[8,128]{1,0:T(8,128)S(1)} %get-tuple-element.31), channel_id=1, source_target_pairs={{0,8},{4,12},{8,0},{12,4},{1,9},{5,13},{9,1},{13,5},{2,10},{6,14},... | collective-permute-start | bytes 12296 | tf_op jit(solution)/shard_map/ppermute | solution.py:296
  132.2 0.0 collective-permute-start.17
  132.2 0.0 collective-permute-done.11.refs_2_
  132.2 1.5 collective-permute-start.3
  133.6 1.8 %collective-permute-start.4 = (bf16[192,1024]{1,0:T(8,128)(2,1)S(1)}, bf16[192,1024]{1,0:T(8,128)(2,1)S(1)}, u32[]{:S(2)}, u32[]{:S(2)}) collective-permute-start(bf16[192,1024]{1,0:T(8,128)(2,1)S(1)} %get-tuple-element.21), channel_id=1, source_target_pairs={{0,8},{4,12},{8,0},{12,4},{1,9},{5,13},{9,1},{13,5},{2,10},{6,14},... | collective-permute-start | bytes 1179656 | tf_op jit(solution)/shard_map/ppermute | solution.py:296
  135.4 0.0 collective-permute-start.5
  135.5 19.3 %grads.3 = (bf16[2048,4096]{1,0:T(8,128)(2,1)}, bf16[768,2048]{1,0:T(8,128)(2,1)}) custom-call(s32[3]{0:T(128)S(1)} %add_add_fusion.j_ref, bf16[768,2048]{1,0:T(8,128)(2,1)} %bitcast.24, bf16[2048,4096]{1,0:T(8,128)(2,1)} %bitcast.18, bf16[192,1024]{1,0:T(8,128)(2,1)} %collective-permute-done.6.refs_0_, ...), custom_call_target="tpu_custom_call", output_to_operand_aliasing={{0}: (8, {})} | custom-call | flops 12884901888 | bytes 26214400 | tf_op jit(solution)/shard_map/grads/pallas_call | solution.py:251
  154.8 0.1 add_reduce_fusion
  154.9 0.6 multiply_reduce_fusion
  156.2 10.3 %collective-permute-done.4.refs_2_ = bf16[192,1024]{1,0:T(8,128)(2,1)S(1)} collective-permute-done((bf16[192,1024]{1,0:T(8,128)(2,1)S(1)}, bf16[192,1024]{1,0:T(8,128)(2,1)S(1)}, u32[]{:S(2)}, u32[]{:S(2)}) %collective-permute-start.4) | collective-permute-done | bytes 393248 | tf_op jit(solution)/shard_map/ppermute | solution.py:296
  166.5 2.5 %collective-permute-done.5.refs_3_ = bf16[192,1024]{1,0:T(8,128)(2,1)S(1)} collective-permute-done((bf16[192,1024]{1,0:T(8,128)(2,1)S(1)}, bf16[192,1024]{1,0:T(8,128)(2,1)S(1)}, u32[]{:S(2)}, u32[]{:S(2)}) %collective-permute-start.5) | collective-permute-done | bytes 393248 | tf_op jit(solution)/shard_map/ppermute | solution.py:296
  169.1 2.0 %mix.1 = bf16[256,1024]{1,0:T(8,128)(2,1)} custom-call(s32[1]{0:T(128)} %bitcast.me_ref, s32[256,2]{1,0:T(8,128)S(1)} %copy.16.ids_ref, f32[256,2]{1,0:T(8,128)S(1)} %copy.17.comb_ref, bf16[192,1024]{1,0:T(8,128)(2,1)S(1)} %get-tuple-element.19.refs_0_, bf16[192,1024]{1,0:T(8,128)(2,1)S(1)} %collective-permute-done.3.refs_1_, ...), custom_call_target="tpu_custom_call" | custom-call | tf_op jit(solution)/shard_map/mix/pallas_call | solution.py:91
  (19 shorter events, 0.0 us)
Async XLA Ops:
  0.6 7.1 %copy-start.1 = (s32[256,2]{0,1:T(2,128)S(1)}, s32[256,2]{0,1:T(2,128)}, u32[]{:S(2)}) copy-start(s32[256,2]{0,1:T(2,128)} %param.8) | copy-start | bytes 6148
  0.7 7.2 %copy-start.2 = (f32[256,2]{0,1:T(2,128)S(1)}, f32[256,2]{0,1:T(2,128)}, u32[]{:S(2)}) copy-start(f32[256,2]{0,1:T(2,128)} %param.9) | copy-start | bytes 6148
  0.7 7.4 %copy-start = (bf16[256,1024]{1,0:T(8,128)(2,1)S(1)}, bf16[256,1024]{1,0:T(8,128)(2,1)}, u32[]{:S(2)}) copy-start(bf16[256,1024]{1,0:T(8,128)(2,1)} %up_ref.1) | copy-start | bytes 1572868
  7.0 21.1 %collective-permute-start.1 = (bf16[768,1024]{1,0:T(8,128)(2,1)S(1)}, bf16[768,1024]{1,0:T(8,128)(2,1)}, u32[]{:S(2)}, u32[]{:S(2)}) collective-permute-start(bf16[768,1024]{1,0:T(8,128)(2,1)S(1)} %forward.3.refs_0_), channel_id=1, source_target_pairs={{0,1},{1,0},{2,3},{3,2},{4,5},{5,4},{6,7},{7,6},{8,9},{9,8},{10,11... | collective-permute-start | bytes 4718600 | tf_op jit(solution)/shard_map/ppermute | solution.py:299
  10.1 21.6 %collective-permute-start.7 = (bf16[192,1024]{1,0:T(8,128)(2,1)}, bf16[192,1024]{1,0:T(8,128)(2,1)}, u32[]{:S(2)}, u32[]{:S(2)}) collective-permute-start(bf16[192,1024]{1,0:T(8,128)(2,1)} %get-tuple-element.24), channel_id=1, source_target_pairs={{0,4},{4,8},{8,12},{12,0},{1,5},{5,9},{9,13},{13,1},{2,6},{6,10},{... | collective-permute-start | bytes 1179656 | tf_op jit(solution)/shard_map/ppermute | solution.py:296
  11.4 34.1 %collective-permute-start.8 = (bf16[192,1024]{1,0:T(8,128)(2,1)}, bf16[192,1024]{1,0:T(8,128)(2,1)}, u32[]{:S(2)}, u32[]{:S(2)}) collective-permute-start(bf16[192,1024]{1,0:T(8,128)(2,1)} %get-tuple-element.25), channel_id=1, source_target_pairs={{0,8},{4,12},{8,0},{12,4},{1,9},{5,13},{9,1},{13,5},{2,10},{6,14},... | collective-permute-start | bytes 1179656 | tf_op jit(solution)/shard_map/ppermute | solution.py:296
  12.4 35.2 %collective-permute-start.9 = (bf16[192,1024]{1,0:T(8,128)(2,1)}, bf16[192,1024]{1,0:T(8,128)(2,1)}, u32[]{:S(2)}, u32[]{:S(2)}) collective-permute-start(bf16[192,1024]{1,0:T(8,128)(2,1)} %get-tuple-element.26), channel_id=1, source_target_pairs={{0,12},{4,0},{8,4},{12,8},{1,13},{5,1},{9,5},{13,9},{2,14},{6,2},{... | collective-permute-start | bytes 1179656 | tf_op jit(solution)/shard_map/ppermute | solution.py:296
  27.2 74.0 %collective-permute-start = (bf16[768,1024]{1,0:T(8,128)(2,1)}, bf16[768,1024]{1,0:T(8,128)(2,1)}, u32[]{:S(2)}, u32[]{:S(2)}) collective-permute-start(bf16[768,1024]{1,0:T(8,128)(2,1)} %forward.5), channel_id=1, source_target_pairs={{0,1},{1,0},{2,3},{3,2},{4,5},{5,4},{6,7},{7,6},{8,9},{9,8},{10,11... | collective-permute-start | bytes 4718600 | tf_op jit(solution)/shard_map/ppermute | solution.py:299
  30.4 71.3 %collective-permute-start.2 = (bf16[768,1024]{1,0:T(8,128)(2,1)S(1)}, bf16[768,1024]{1,0:T(8,128)(2,1)}, u32[]{:S(2)}, u32[]{:S(2)}) collective-permute-start(bf16[768,1024]{1,0:T(8,128)(2,1)S(1)} %add.75), channel_id=1, source_target_pairs={{0,2},{1,3},{2,0},{3,1},{4,6},{5,7},{6,4},{7,5},{8,10},{9,11},{10,... | collective-permute-start | bytes 4718600 | tf_op jit(solution)/shard_map/ppermute | solution.py:302
  48.7 52.5 %collective-permute-start.10 = (bf16[576,1024]{1,0:T(8,128)(2,1)S(1)}, bf16[576,1024]{1,0:T(8,128)(2,1)}, u32[]{:S(2)}, u32[]{:S(2)}) collective-permute-start(bf16[576,1024]{1,0:T(8,128)(2,1)S(1)} %constant_dynamic-update-slice_fusion.refs_1_), channel_id=1, source_target_pairs={{0,2},{1,3},{2,0},{3,1},{4,6},{5,7},{6,4},{7,5},{8,10},{9,11},{10,... | collective-permute-start | bytes 3538952 | tf_op jit(solution)/shard_map/ppermute | solution.py:302
  50.0 59.7 %collective-permute-start.14 = (bf16[576,1024]{1,0:T(8,128)(2,1)S(1)}, bf16[576,1024]{1,0:T(8,128)(2,1)}, u32[]{:S(2)}, u32[]{:S(2)}) collective-permute-start(bf16[576,1024]{1,0:T(8,128)(2,1)S(1)} %constant_dynamic-update-slice_fusion.refs_1_), channel_id=1, source_target_pairs={{0,1},{1,0},{2,3},{3,2},{4,5},{5,4},{6,7},{7,6},{8,9},{9,8},{10,11... | collective-permute-start | bytes 3538952 | tf_op jit(solution)/shard_map/ppermute | solution.py:299
  50.7 49.6 %collective-permute-start.6 = (bf16[192,1024]{1,0:T(8,128)(2,1)}, bf16[192,1024]{1,0:T(8,128)(2,1)}, u32[]{:S(2)}, u32[]{:S(2)}) collective-permute-start(bf16[192,1024]{1,0:T(8,128)(2,1)} %get-tuple-element.23.refs_0_), channel_id=1, source_target_pairs={{0,2},{1,3},{2,0},{3,1},{4,6},{5,7},{6,4},{7,5},{8,10},{9,11},{10,... | collective-permute-start | bytes 1179656 | tf_op jit(solution)/shard_map/ppermute | solution.py:302
  100.3 9.4 %collective-permute-start.13 = (bf16[192,1024]{1,0:T(8,128)(2,1)}, bf16[192,1024]{1,0:T(8,128)(2,1)S(1)}, u32[]{:S(2)}, u32[]{:S(2)}) collective-permute-start(bf16[192,1024]{1,0:T(8,128)(2,1)} %get-tuple-element.23.refs_0_), channel_id=1, source_target_pairs={{0,1},{1,0},{2,3},{3,2},{4,5},{5,4},{6,7},{7,6},{8,9},{9,8},{10,11... | collective-permute-start | bytes 1179656 | tf_op jit(solution)/shard_map/ppermute | solution.py:299
  101.2 31.0 %collective-permute-start.11 = (bf16[192,1024]{1,0:T(8,128)(2,1)}, bf16[192,1024]{1,0:T(8,128)(2,1)S(1)}, u32[]{:S(2)}, u32[]{:S(2)}) collective-permute-start(bf16[192,1024]{1,0:T(8,128)(2,1)} %collective-permute-done.6.refs_0_), channel_id=1, source_target_pairs={{0,1},{1,0},{2,3},{3,2},{4,5},{5,4},{6,7},{7,6},{8,9},{9,8},{10,11... | collective-permute-start | bytes 1179656 | tf_op jit(solution)/shard_map/ppermute | solution.py:299
  101.2 32.4 %collective-permute-start.12 = (bf16[576,1024]{1,0:T(8,128)(2,1)}, bf16[576,1024]{1,0:T(8,128)(2,1)S(1)}, u32[]{:S(2)}, u32[]{:S(2)}) collective-permute-start(bf16[576,1024]{1,0:T(8,128)(2,1)} %collective-permute-done.10.refs_1_), channel_id=1, source_target_pairs={{0,1},{1,0},{2,3},{3,2},{4,5},{5,4},{6,7},{7,6},{8,9},{9,8},{10,11... | collective-permute-start | bytes 3538952 | tf_op jit(solution)/shard_map/ppermute | solution.py:299
  109.6 25.8 %collective-permute-start.15 = (f32[8,128]{1,0:T(8,128)S(1)}, f32[8,128]{1,0:T(8,128)S(1)}, u32[]{:S(2)}, u32[]{:S(2)}) collective-permute-start(f32[8,128]{1,0:T(8,128)S(1)} %get-tuple-element.31), channel_id=1, source_target_pairs={{0,4},{4,8},{8,12},{12,0},{1,5},{5,9},{9,13},{13,1},{2,6},{6,10},{... | collective-permute-start | bytes 12296 | tf_op jit(solution)/shard_map/ppermute | solution.py:296
  129.0 25.8 %collective-permute-start.16 = (f32[8,128]{1,0:T(8,128)S(1)}, f32[8,128]{1,0:T(8,128)S(1)}, u32[]{:S(2)}, u32[]{:S(2)}) collective-permute-start(f32[8,128]{1,0:T(8,128)S(1)} %get-tuple-element.31), channel_id=1, source_target_pairs={{0,8},{4,12},{8,0},{12,4},{1,9},{5,13},{9,1},{13,5},{2,10},{6,14},... | collective-permute-start | bytes 12296 | tf_op jit(solution)/shard_map/ppermute | solution.py:296
  132.2 22.6 %collective-permute-start.17 = (f32[8,128]{1,0:T(8,128)S(1)}, f32[8,128]{1,0:T(8,128)S(1)}, u32[]{:S(2)}, u32[]{:S(2)}) collective-permute-start(f32[8,128]{1,0:T(8,128)S(1)} %get-tuple-element.31), channel_id=1, source_target_pairs={{0,12},{4,0},{8,4},{12,8},{1,13},{5,1},{9,5},{13,9},{2,14},{6,2},{... | collective-permute-start | bytes 12296 | tf_op jit(solution)/shard_map/ppermute | solution.py:296
  132.2 24.0 %collective-permute-start.3 = (bf16[192,1024]{1,0:T(8,128)(2,1)S(1)}, bf16[192,1024]{1,0:T(8,128)(2,1)S(1)}, u32[]{:S(2)}, u32[]{:S(2)}) collective-permute-start(bf16[192,1024]{1,0:T(8,128)(2,1)S(1)} %get-tuple-element.20), channel_id=1, source_target_pairs={{0,4},{4,8},{8,12},{12,0},{1,5},{5,9},{9,13},{13,1},{2,6},{6,10},{... | collective-permute-start | bytes 1179656 | tf_op jit(solution)/shard_map/ppermute | solution.py:296
  133.6 32.9 %collective-permute-start.4 = (bf16[192,1024]{1,0:T(8,128)(2,1)S(1)}, bf16[192,1024]{1,0:T(8,128)(2,1)S(1)}, u32[]{:S(2)}, u32[]{:S(2)}) collective-permute-start(bf16[192,1024]{1,0:T(8,128)(2,1)S(1)} %get-tuple-element.21), channel_id=1, source_target_pairs={{0,8},{4,12},{8,0},{12,4},{1,9},{5,13},{9,1},{13,5},{2,10},{6,14},... | collective-permute-start | bytes 1179656 | tf_op jit(solution)/shard_map/ppermute | solution.py:296
  135.4 33.6 %collective-permute-start.5 = (bf16[192,1024]{1,0:T(8,128)(2,1)S(1)}, bf16[192,1024]{1,0:T(8,128)(2,1)S(1)}, u32[]{:S(2)}, u32[]{:S(2)}) collective-permute-start(bf16[192,1024]{1,0:T(8,128)(2,1)S(1)} %get-tuple-element.22), channel_id=1, source_target_pairs={{0,12},{4,0},{8,4},{12,8},{1,13},{5,1},{9,5},{13,9},{2,14},{6,2},{... | collective-permute-start | bytes 1179656 | tf_op jit(solution)/shard_map/ppermute | solution.py:296

commit v3 on v2

--- a/solution.py
+++ b/solution.py
@@ -73,7 +73,7 @@
 
 def mix_kernel(experts_all, capacity, me_ref, ids_ref, comb_ref, *refs):
     me = me_ref[0]
-    out_ref = refs[experts_all]
+    out_ref = refs[-1]
     named, weight, slot = token_table(ids_ref[...], comb_ref[...], experts_all)
     total = None
     for s in range(experts_all):
@@ -85,17 +85,18 @@
     out_ref[...] = total.astype(BF16)
 
 
-def mix(me, ids, combine, returned, experts_all, capacity):
+def mix(me, ids, combine, returned, experts_all, capacity, after=()):
     width = returned[0].shape[1]
     vmem = pl.BlockSpec(memory_space=pltpu.VMEM)
     return pl.pallas_call(
         functools.partial(mix_kernel, experts_all, capacity),
         out_shape=jax.ShapeDtypeStruct((ids.shape[0], width), BF16),
-        in_specs=[pl.BlockSpec(memory_space=pltpu.SMEM)] + [vmem] * (2 + experts_all),
+        in_specs=[pl.BlockSpec(memory_space=pltpu.SMEM)] + [vmem] * (2 + experts_all)
+        + [pl.BlockSpec(memory_space=pl.ANY)] * len(after),
         out_specs=vmem,
         compiler_params=pltpu.CompilerParams(vmem_limit_bytes=VMEM_LIMIT),
         name="mix",
-    )(me, ids, combine, *returned)
+    )(me, ids, combine, *returned, *after)
 
 
 def cost(rows, depth, columns):
@@ -146,7 +147,7 @@
 
 
 def last_forward_kernel(extras, experts_all, capacity, j_ref, hidden_ref, w_ref, *refs):
-    outs, scratch = refs[extras + 1 : -1], refs[-1]
+    outs, scratch = refs[-experts_all - 2 : -1], refs[-1]
     total = jnp.dot(hidden_ref[...], w_ref[...], preferred_element_type=F32)
     for extra in refs[:extras]:
         total = total + extra[...].astype(F32)
@@ -157,7 +158,7 @@
     outs[experts_all][...] = refs[extras][...]
 
 
-def last_forward_block(block, hidden, weight, width, extras, stats, experts_all):
+def last_forward_block(block, hidden, weight, width, extras, stats, experts_all, after=()):
     rows, depth = hidden.shape
     capacity = rows // experts_all
     tile = tile_of(width, 512)
@@ -175,7 +176,8 @@
                 pl.BlockSpec((depth, tile), lambda i, j: (0, j[0] * tiles + i)),
             ]
             + [pl.BlockSpec((rows, tile), lambda i, j: (0, i))] * len(extras)
-            + [stats_spec],
+            + [stats_spec]
+            + [pl.BlockSpec(memory_space=pl.ANY)] * len(after),
             out_specs=[pl.BlockSpec((capacity, tile), lambda i, j: (0, i))] * experts_all
             + [stats_spec],
             scratch_shapes=[pltpu.VMEM((rows, tile), BF16)],
@@ -183,7 +185,41 @@
         cost_estimate=cost(rows, depth, width),
         compiler_params=pltpu.CompilerParams(vmem_limit_bytes=VMEM_LIMIT),
         name="last_forward",
-    )(block, hidden, weight, *extras, stats)
+    )(block, hidden, weight, *extras, stats, *after)
+
+
+def join_kernel(parts, *refs):
+    capacity = refs[0].shape[0]
+    for n in range(parts):
+        refs[-1][n * capacity : (n + 1) * capacity, :] = refs[n][...]
+
+
+def join(parts, after):
+    capacity, width = parts[0].shape
+    vmem = pl.BlockSpec(memory_space=pltpu.VMEM)
+    return pl.pallas_call(
+        functools.partial(join_kernel, len(parts)),
+        out_shape=jax.ShapeDtypeStruct((len(parts) * capacity, width), BF16),
+        in_specs=[vmem] * len(parts) + [pl.BlockSpec(memory_space=pl.ANY)],
+        out_specs=vmem,
+        name="join",
+    )(*parts, after)
+
+
+def hold_kernel(*refs):
+    pass
+
+
+def hold(x, after):
+    anywhere = pl.BlockSpec(memory_space=pl.ANY)
+    return pl.pallas_call(
+        hold_kernel,
+        out_shape=jax.ShapeDtypeStruct(x.shape, x.dtype),
+        in_specs=[anywhere, anywhere],
+        out_specs=anywhere,
+        input_output_aliases={0: 0},
+        name="hold",
+    )(x, after)
 
 
 def add_kernel(a_ref, b_ref, out_ref):
@@ -237,7 +273,7 @@
     out_h[...] = total.astype(out_h.dtype)
 
 
-def grads(place, hidden, weight, pieces, experts_all, before, last):
+def grads(place, hidden, weight, pieces, experts_all, before, last, after=()):
     rows, depth = hidden.shape
     model = weight.shape[1]
     width = pieces[0].shape[1]
@@ -262,7 +298,8 @@
                 pl.BlockSpec((tile_h, chip_width), lambda i, j: (i, j[0])),
             ]
             + [whole(x) for x in pieces]
-            + ([] if first else [h_spec, pl.BlockSpec(memory_space=pl.ANY)]),
+            + ([] if first else [h_spec, pl.BlockSpec(memory_space=pl.ANY)])
+            + [pl.BlockSpec(memory_space=pl.ANY)] * len(after),
             out_specs=[
                 pl.BlockSpec((depth, tile_w), lambda i, j: (0, j[0] * steps + i)),
                 h_spec,
@@ -273,7 +310,7 @@
         cost_estimate=cost(rows, depth, 2 * chip_width),
         compiler_params=pltpu.CompilerParams(vmem_limit_bytes=VMEM_LIMIT),
         name="grads",
-    )(place, hidden, weight, *pieces, *extra)
+    )(place, hidden, weight, *pieces, *extra, *after)
 
 
 def on_device(hidden, w_down, upstream, expert_ids, combine):
@@ -304,39 +341,44 @@
     *routed, stats = route(me_ref, expert_ids, combine, upstream, experts_all, capacity)
     own_rows = routed[0]
     own_at = [to_chip(own_rows, d) if d else own_rows for d in range(chips)]
-    far_rows = jnp.concatenate([to_expert(routed[s], s) for s in range(1, experts_all)], axis=0)
-
-    arrived, after = [], ()
+    far_parts = [to_expert(routed[s], s) for s in range(1, experts_all)]
+
+    arrived, after = [], (stats,)
     for d in range(1, chips):
         mine = lax.rem(here + 2 * d, et)
         other = mine + 1 - 2 * core
         sent = forward_block(other.reshape(1), hidden_local, weight_local, width, (), after)
         block = forward_block(mine.reshape(1), hidden_local, weight_local, width, (), (sent,))
-        after = (block,)
-        arrived.append(to_chip(add(block, to_core(sent)), d))
+        summed = add(block, to_core(sent))
+        after = (summed, own_at[d])
+        arrived.append(to_chip(summed, d))
     other = here + 1 - 2 * core
-    sent = to_core(forward_block(other.reshape(1), hidden_local, weight_local, width, (), after))
+    block = forward_block(other.reshape(1), hidden_local, weight_local, width, (), after)
+    sent = to_core(block)
+    far_rows = join(far_parts, block)
 
     far_at = [to_chip(far_rows, d) if d else far_rows for d in range(chips)]
-    gradients = None
-    results = None
+    gradients, results, after = None, None, ()
     for d in range(chips):
         chip = lax.rem(here // 2 - d + chips, chips)
-        pieces = [own_at[d], far_at[d], to_core(own_at[d]), to_core(far_at[d])]
+        far = hold(far_at[d], gradients[1] if d > 1 else results[-1]) if d else far_at[d]
+        pieces = [own_at[d], far, to_core(own_at[d]), to_core(far)]
         place = jnp.stack([chip, core, me])
         gradients = grads(
-            place, hidden_local, weight_local, pieces, experts_all, gradients, d == chips - 1
+            place, hidden_local, weight_local, pieces, experts_all, gradients, d == chips - 1, after
         )
         if d == 0:
             results = last_forward_block(
-                jnp.stack([here, me]), hidden_local, weight_local, width, [sent, *arrived], stats, experts_all
+                jnp.stack([here, me]), hidden_local, weight_local, width, [sent, *arrived], stats, experts_all,
+                (gradients[1],),
             )
+            after = (results[-1],)
     grad_w, grad_h = gradients
 
     *result, stats_late = results
     returned = [result[0]] + [to_expert(result[s], s) for s in range(1, experts_all)]
     all_stats = [stats_late] + [to_expert(stats_late, s) for s in range(1, experts_all)]
-    mixed = mix(me_ref, expert_ids, combine, returned, experts_all, capacity)
+    mixed = mix(me_ref, expert_ids, combine, returned, experts_all, capacity, (grad_h,))
 
     table = sum(
         jnp.where(

time: 173 us -> 161 us (0.931)
  waiting for transfers between devices: 76 us -> 59.6 us
  local copies, waits for them, and re-layouts: 3.35 us -> 6.42 us
  Pallas kernels: 72.6 us -> 74.9 us
    ppermute x3, waiting for transfers between devices: 49.2 us -> 27.4 us  [to_chip(): return lax.ppermute(x, 'et', [(i, (i + 2 * d) % et) for i in range(et)])]
    unnamed x10 -> x18, local copies, waits for them, and re-layouts: 2.32 us -> 6.42 us
    ppermute x9, waiting for transfers between devices: 26.8 us -> 30.3 us  [to_expert(): lax.ppermute(x, 'ep', [(i, (i + s) % experts_all) for i in range(experts_...]
    pallas_call x0 -> x2, Pallas kernels: none -> 2.36 us  [the longest x1 2.36 us: join(): pl.pallas_call(functools.partial(join_kernel, len(parts)), out_shape=jax....]
    ppermute x6, waiting for transfers between devices: 0.02 us -> 1.82 us  [to_core(): return lax.ppermute(x, 'et', [(i, i ^ 1) for i in range(et)])]
  transfers between devices with their start and end apart: 18 -> 18, of which waited for: 5 -> 7; matrix products, arithmetic and copies ran while one was open for 2% -> 1% of each run, Pallas kernels for 37% -> 39%
where the time goes in v3:
time: 161 us
  Pallas kernels  74.9 us (47%)
  waiting for transfers between devices  59.6 us (37%)
  starting transfers between devices  16.3 us (10%)
  local copies, waits for them, and re-layouts  6.42 us (4%)
  between operations  2.6 us (2%)
    pallas_call x2, Pallas kernels, grads(): pl.pallas_call(functools.partial(grads_kernel, experts_all, first, last,...  38.7 us
    ppermute x9, waiting for transfers between devices, to_expert(): lax.ppermute(x, 'ep', [(i, (i + s) % experts_all) for i in range(experts_...  30.3 us
    ppermute x3, waiting for transfers between devices, to_chip(): return lax.ppermute(x, 'et', [(i, (i + 2 * d) % et) for i in range(et)])  27.4 us
    pallas_call x3, Pallas kernels, forward_block(): pl.pallas_call(functools.partial(forward_kernel, len(extras)), out_shape=...  18.7 us
    ppermute x9, starting transfers between devices, to_expert(): lax.ppermute(x, 'ep', [(i, (i + s) % experts_all) for i in range(experts_...  11 us
    pallas_call x1, Pallas kernels, last_forward_block(): pl.pallas_call(functools.partial(last_forward_kernel, len(extras), expert...  8.59 us
    unnamed x18, local copies, waits for them, and re-layouts  6.42 us
  transfers between devices with their start and end apart: 18, of which 7 were waited for; matrix products, arithmetic and copies ran while one was open for 1% of the time, Pallas kernels for 39%

profile of v3, /device:TPU:9, one launch (start us, length us, event | category | flops | bytes accessed | tf_op | source)
XLA Modules:
  0.0 160.7 jit_solution(16771254003667171023)
XLA Ops:
  0.6 0.8 copy.17.ids_ref
  1.5 0.8 copy.18.comb_ref
  2.3 0.0 copy-start.3
  2.3 1.0 copy-done.3
  3.3 2.1 %route.1 = (bf16[192,1024]{1,0:T(8,128)(2,1)}, bf16[192,1024]{1,0:T(8,128)(2,1)}, bf16[192,1024]{1,0:T(8,128)(2,1)}, bf16[192,1024]{1,0:T(8,128)(2,1)}, f32[8,128]{1,0:T(8,128)S(1)}) custom-call(s32[1]{0:T(128)} %bitcast.me_ref, s32[256,2]{1,0:T(8,128)S(1)} %copy.17.ids_ref, f32[256,2]{1,0:T(8,128)S(1)} %copy.18.comb_ref, bf16[256,1024]{1,0:T(8,128)(2,1)S(1)} %copy-done.3), custom_call_target="tpu_custom_call" | custom-call | tf_op jit(solution)/shard_map/route/pallas_call | solution.py:63
  5.4 6.2 %forward.3.refs_0_ = bf16[768,1024]{1,0:T(8,128)(2,1)S(1)} custom-call(s32[1]{0:T(128)} %bitcast.6.j_ref, bf16[768,2048]{1,0:T(8,128)(2,1)} %bitcast.19, bf16[2048,4096]{1,0:T(8,128)(2,1)} %bitcast.13, f32[8,128]{1,0:T(8,128)S(1)} %get-tuple-element.18.refs_0_.refs_2_), custom_call_target="tpu_custom_call" | custom-call | flops 3221225472 | bytes 8912896 | tf_op jit(solution)/shard_map/forward/pallas_call | solution.py:129
  11.6 0.7 collective-permute-start
  12.4 1.2 collective-permute-start.1
  13.6 1.3 collective-permute-start.4
  14.9 1.0 collective-permute-start.5
  15.9 1.5 collective-permute-start.6
  17.4 6.2 %forward.4.a_ref = bf16[768,1024]{1,0:T(8,128)(2,1)S(1)} custom-call(s32[1]{0:T(128)} %bitcast.5.j_ref, bf16[768,2048]{1,0:T(8,128)(2,1)} %bitcast.20, bf16[2048,4096]{1,0:T(8,128)(2,1)} %bitcast.14, bf16[768,1024]{1,0:T(8,128)(2,1)S(1)} %forward.3.refs_0_), custom_call_target="tpu_custom_call" | custom-call | flops 3221225472 | bytes 8912896 | tf_op jit(solution)/shard_map/forward/pallas_call | solution.py:129
  23.7 2.4 %add.75.refs_0_ = bf16[768,1024]{1,0:T(8,128)(2,1)S(1)} custom-call(bf16[768,1024]{1,0:T(8,128)(2,1)S(1)} %forward.4.a_ref, bf16[768,1024]{1,0:T(8,128)(2,1)} %collective-permute-done.b_ref), custom_call_target="tpu_custom_call" | custom-call | tf_op jit(solution)/shard_map/add/pallas_call | solution.py:232
  26.1 6.3 %forward.5.refs_3_ = bf16[768,1024]{1,0:T(8,128)(2,1)S(1)} custom-call(s32[1]{0:T(128)} %bitcast.4.j_ref, bf16[768,2048]{1,0:T(8,128)(2,1)} %bitcast.21, bf16[2048,4096]{1,0:T(8,128)(2,1)} %bitcast.15, bf16[768,1024]{1,0:T(8,128)(2,1)S(1)} %add.75.refs_0_, bf16[192,1024]{1,0:T(8,128)(2,1)} %collective-permute-done.1.refs_1_.refs_0_), custom_call_target="tpu_custom_call" | custom-call | flops 3221225472 | bytes 8912896 | tf_op jit(solution)/shard_map/forward/pallas_call | solution.py:129
  32.3 1.1 copy-done
  33.5 15.2 %collective-permute-done.5.refs_1_ = bf16[192,1024]{1,0:T(8,128)(2,1)} collective-permute-done((bf16[192,1024]{1,0:T(8,128)(2,1)}, bf16[192,1024]{1,0:T(8,128)(2,1)}, u32[]{:S(2)}, u32[]{:S(2)}) %collective-permute-start.5) | collective-permute-done | bytes 393248 | tf_op jit(solution)/shard_map/ppermute | solution.py:333
  48.7 2.5 %collective-permute-done.6.refs_2_ = bf16[192,1024]{1,0:T(8,128)(2,1)} collective-permute-done((bf16[192,1024]{1,0:T(8,128)(2,1)}, bf16[192,1024]{1,0:T(8,128)(2,1)}, u32[]{:S(2)}, u32[]{:S(2)}) %collective-permute-start.6) | collective-permute-done | bytes 393248 | tf_op jit(solution)/shard_map/ppermute | solution.py:333
  51.2 2.4 %join.1.refs_1_ = bf16[576,1024]{1,0:T(8,128)(2,1)} custom-call(bf16[192,1024]{1,0:T(8,128)(2,1)} %collective-permute-done.4.refs_0_, bf16[192,1024]{1,0:T(8,128)(2,1)} %collective-permute-done.5.refs_1_, bf16[192,1024]{1,0:T(8,128)(2,1)} %collective-permute-done.6.refs_2_, bf16[768,1024]{1,0:T(8,128)(2,1)} %copy-done), custom_call_target="tpu_custom_call" | custom-call | tf_op jit(solution)/shard_map/join/pallas_call | solution.py:200
  53.5 0.5 collective-permute-start.8
  54.0 0.0 collective-permute-start.7
  54.0 0.5 collective-permute-start.2
  54.5 0.2 collective-permute-start.3
  54.8 0.1 pad_add_fusion.j_ref
  54.8 0.1 add_add_fusion.j_ref
  54.9 1.2 collective-permute-start.12
  56.1 1.8 %collective-permute-done.7.refs_2_ = bf16[192,1024]{1,0:T(8,128)(2,1)} collective-permute-done((bf16[192,1024]{1,0:T(8,128)(2,1)}, bf16[192,1024]{1,0:T(8,128)(2,1)}, u32[]{:S(2)}, u32[]{:S(2)}) %collective-permute-start.7) | collective-permute-done | bytes 393248 | tf_op jit(solution)/shard_map/ppermute | solution.py:336
  58.0 1.3 copy-done.2
  59.2 19.3 %grads.2 = (bf16[2048,4096]{1,0:T(8,128)(2,1)}, f32[768,2048]{1,0:T(8,128)}) custom-call(s32[3]{0:T(128)S(1)} %add_add_fusion.j_ref, bf16[768,2048]{1,0:T(8,128)(2,1)} %bitcast.22, bf16[2048,4096]{1,0:T(8,128)(2,1)} %bitcast.16, bf16[192,1024]{1,0:T(8,128)(2,1)} %get-tuple-element.19.refs_0_, bf16[576,1024]{1,0:T(8,128)(2,1)S(1)} %copy-done.2, ...), custom_call_target="tpu_custom_call" | custom-call | flops 12884901888 | bytes 26214400 | tf_op jit(solution)/shard_map/grads/pallas_call | solution.py:287
  78.6 12.1 %collective-permute-done.3.refs_1_ = bf16[768,1024]{1,0:T(8,128)(2,1)} collective-permute-done((bf16[768,1024]{1,0:T(8,128)(2,1)S(1)}, bf16[768,1024]{1,0:T(8,128)(2,1)}, u32[]{:S(2)}, u32[]{:S(2)}) %collective-permute-start.3) | collective-permute-done | bytes 1572896 | tf_op jit(solution)/shard_map/ppermute | solution.py:339
  90.6 8.6 %last_forward.1 = (bf16[192,1024]{1,0:T(8,128)(2,1)S(1)}, bf16[192,1024]{1,0:T(8,128)(2,1)}, bf16[192,1024]{1,0:T(8,128)(2,1)}, bf16[192,1024]{1,0:T(8,128)(2,1)S(1)}, f32[8,128]{1,0:T(8,128)S(1)}) custom-call(s32[2]{0:T(128)S(1)} %pad_add_fusion.j_ref, bf16[768,2048]{1,0:T(8,128)(2,1)} %bitcast.23, bf16[2048,4096]{1,0:T(8,128)(2,1)} %bitcast.17, ...), custom_call_target="tpu_custom_call" | custom-call | flops 3221225472 | bytes 8912896 | tf_op jit(solution)/shard_map/last_forward/pallas_call | solution.py:167
  99.2 0.6 copy-done.4
  99.8 0.7 copy-done.6
  100.6 15.3 %collective-permute-done.12.refs_0_ = bf16[576,1024]{1,0:T(8,128)(2,1)} collective-permute-done((bf16[576,1024]{1,0:T(8,128)(2,1)}, bf16[576,1024]{1,0:T(8,128)(2,1)}, u32[]{:S(2)}, u32[]{:S(2)}) %collective-permute-start.12) | collective-permute-done | bytes 1179680 | tf_op jit(solution)/shard_map/ppermute | solution.py:339
  115.9 0.8 collective-permute-start.14
  116.7 0.1 collective-permute-start.13
  116.8 0.0 collective-permute-start.17
  116.9 1.4 collective-permute-start.16
  118.3 2.3 %collective-permute-start.15 = (f32[8,128]{1,0:T(8,128)S(1)}, f32[8,128]{1,0:T(8,128)S(1)}, u32[]{:S(2)}, u32[]{:S(2)}) collective-permute-start(f32[8,128]{1,0:T(8,128)S(1)} %copy-done.5), channel_id=1, source_target_pairs={{0,4},{4,8},{8,12},{12,0},{1,5},{5,9},{9,13},{13,1},{2,6},{6,10},{... | collective-permute-start | bytes 12296 | tf_op jit(solution)/shard_map/ppermute | solution.py:333
  120.5 0.1 add_add_fusion.1.j_ref
  120.6 0.0 collective-permute-start.9
  120.7 1.8 %collective-permute-start.10 = (bf16[192,1024]{1,0:T(8,128)(2,1)}, bf16[192,1024]{1,0:T(8,128)(2,1)S(1)}, u32[]{:S(2)}, u32[]{:S(2)}) collective-permute-start(bf16[192,1024]{1,0:T(8,128)(2,1)} %get-tuple-element.26), channel_id=1, source_target_pairs={{0,8},{4,12},{8,0},{12,4},{1,9},{5,13},{9,1},{13,5},{2,10},{6,14},... | collective-permute-start | bytes 1179656 | tf_op jit(solution)/shard_map/ppermute | solution.py:333
  122.5 1.6 %collective-permute-start.11 = (bf16[192,1024]{1,0:T(8,128)(2,1)S(1)}, bf16[192,1024]{1,0:T(8,128)(2,1)S(1)}, u32[]{:S(2)}, u32[]{:S(2)}) collective-permute-start(bf16[192,1024]{1,0:T(8,128)(2,1)S(1)} %copy-done.7), channel_id=1, source_target_pairs={{0,12},{4,0},{8,4},{12,8},{1,13},{5,1},{9,5},{13,9},{2,14},{6,2},{... | collective-permute-start | bytes 1179656 | tf_op jit(solution)/shard_map/ppermute | solution.py:333
  124.1 0.1 add_reduce_fusion
  124.2 0.6 multiply_reduce_fusion
  125.5 19.4 %grads.3 = (bf16[2048,4096]{1,0:T(8,128)(2,1)}, bf16[768,2048]{1,0:T(8,128)(2,1)}) custom-call(s32[3]{0:T(128)S(1)} %add_add_fusion.1.j_ref, bf16[768,2048]{1,0:T(8,128)(2,1)} %bitcast.24, bf16[2048,4096]{1,0:T(8,128)(2,1)} %bitcast.18, bf16[192,1024]{1,0:T(8,128)(2,1)} %collective-permute-done.1.refs_1_.refs_0_, ...), custom_call_target="tpu_custom_call", output_to_operand_aliasing={{0}: (8, {})} | custom-call | flops 12884901888 | bytes 26214400 | tf_op jit(solution)/shard_map/grads/pallas_call | solution.py:287
  144.9 8.7 %collective-permute-done.10.refs_2_ = bf16[192,1024]{1,0:T(8,128)(2,1)S(1)} collective-permute-done((bf16[192,1024]{1,0:T(8,128)(2,1)}, bf16[192,1024]{1,0:T(8,128)(2,1)S(1)}, u32[]{:S(2)}, u32[]{:S(2)}) %collective-permute-start.10) | collective-permute-done | bytes 393248 | tf_op jit(solution)/shard_map/ppermute | solution.py:333
  153.6 4.0 %collective-permute-done.11.refs_3_ = bf16[192,1024]{1,0:T(8,128)(2,1)S(1)} collective-permute-done((bf16[192,1024]{1,0:T(8,128)(2,1)S(1)}, bf16[192,1024]{1,0:T(8,128)(2,1)S(1)}, u32[]{:S(2)}, u32[]{:S(2)}) %collective-permute-start.11) | collective-permute-done | bytes 393248 | tf_op jit(solution)/shard_map/ppermute | solution.py:333
  157.6 2.0 %mix.1 = bf16[256,1024]{1,0:T(8,128)(2,1)} custom-call(s32[1]{0:T(128)} %bitcast.me_ref, s32[256,2]{1,0:T(8,128)S(1)} %copy.17.ids_ref, f32[256,2]{1,0:T(8,128)S(1)} %copy.18.comb_ref, bf16[192,1024]{1,0:T(8,128)(2,1)S(1)} %get-tuple-element.24.refs_0_, bf16[192,1024]{1,0:T(8,128)(2,1)S(1)} %collective-permute-done.9.refs_1_, ...), custom_call_target="tpu_custom_call" | custom-call | tf_op jit(solution)/shard_map/mix/pallas_call | solution.py:91
  (28 shorter events, 0.1 us)
Async XLA Ops:
  2.3 1.0 copy-start.3
  11.6 12.0 %collective-permute-start = (bf16[768,1024]{1,0:T(8,128)(2,1)S(1)}, bf16[768,1024]{1,0:T(8,128)(2,1)}, u32[]{:S(2)}, u32[]{:S(2)}) collective-permute-start(bf16[768,1024]{1,0:T(8,128)(2,1)S(1)} %forward.3.refs_0_), channel_id=1, source_target_pairs={{0,1},{1,0},{2,3},{3,2},{4,5},{5,4},{6,7},{7,6},{8,9},{9,8},{10,11... | collective-permute-start | bytes 4718600 | tf_op jit(solution)/shard_map/ppermute | solution.py:336
  12.4 13.7 %collective-permute-start.1 = (bf16[192,1024]{1,0:T(8,128)(2,1)}, bf16[192,1024]{1,0:T(8,128)(2,1)}, u32[]{:S(2)}, u32[]{:S(2)}) collective-permute-start(bf16[192,1024]{1,0:T(8,128)(2,1)} %get-tuple-element.19.refs_0_), channel_id=1, source_target_pairs={{0,2},{1,3},{2,0},{3,1},{4,6},{5,7},{6,4},{7,5},{8,10},{9,11},{10,... | collective-permute-start | bytes 1179656 | tf_op jit(solution)/shard_map/ppermute | solution.py:339
  13.6 19.8 %collective-permute-start.4 = (bf16[192,1024]{1,0:T(8,128)(2,1)}, bf16[192,1024]{1,0:T(8,128)(2,1)}, u32[]{:S(2)}, u32[]{:S(2)}) collective-permute-start(bf16[192,1024]{1,0:T(8,128)(2,1)} %get-tuple-element.20), channel_id=1, source_target_pairs={{0,4},{4,8},{8,12},{12,0},{1,5},{5,9},{9,13},{13,1},{2,6},{6,10},{... | collective-permute-start | bytes 1179656 | tf_op jit(solution)/shard_map/ppermute | solution.py:333
  14.9 33.8 %collective-permute-start.5 = (bf16[192,1024]{1,0:T(8,128)(2,1)}, bf16[192,1024]{1,0:T(8,128)(2,1)}, u32[]{:S(2)}, u32[]{:S(2)}) collective-permute-start(bf16[192,1024]{1,0:T(8,128)(2,1)} %get-tuple-element.21), channel_id=1, source_target_pairs={{0,8},{4,12},{8,0},{12,4},{1,9},{5,13},{9,1},{13,5},{2,10},{6,14},... | collective-permute-start | bytes 1179656 | tf_op jit(solution)/shard_map/ppermute | solution.py:333
  15.9 35.2 %collective-permute-start.6 = (bf16[192,1024]{1,0:T(8,128)(2,1)}, bf16[192,1024]{1,0:T(8,128)(2,1)}, u32[]{:S(2)}, u32[]{:S(2)}) collective-permute-start(bf16[192,1024]{1,0:T(8,128)(2,1)} %get-tuple-element.22), channel_id=1, source_target_pairs={{0,12},{4,0},{8,4},{12,8},{1,13},{5,1},{9,5},{13,9},{2,14},{6,2},{... | collective-permute-start | bytes 1179656 | tf_op jit(solution)/shard_map/ppermute | solution.py:333
  32.3 1.1 copy-start
  33.5 20.6 %copy-start.1 = (bf16[768,1024]{1,0:T(8,128)(2,1)S(1)}, bf16[768,1024]{1,0:T(8,128)(2,1)}, u32[]{:S(2)}) copy-start(bf16[768,1024]{1,0:T(8,128)(2,1)} %copy-done) | copy-start | bytes 4718596
  53.5 4.4 %collective-permute-start.8 = (bf16[576,1024]{1,0:T(8,128)(2,1)}, bf16[576,1024]{1,0:T(8,128)(2,1)}, u32[]{:S(2)}, u32[]{:S(2)}) collective-permute-start(bf16[576,1024]{1,0:T(8,128)(2,1)} %join.1.refs_1_), channel_id=1, source_target_pairs={{0,1},{1,0},{2,3},{3,2},{4,5},{5,4},{6,7},{7,6},{8,9},{9,8},{10,11... | collective-permute-start | bytes 3538952 | tf_op jit(solution)/shard_map/ppermute | solution.py:336
  54.0 3.9 %collective-permute-start.7 = (bf16[192,1024]{1,0:T(8,128)(2,1)}, bf16[192,1024]{1,0:T(8,128)(2,1)}, u32[]{:S(2)}, u32[]{:S(2)}) collective-permute-start(bf16[192,1024]{1,0:T(8,128)(2,1)} %get-tuple-element.19.refs_0_), channel_id=1, source_target_pairs={{0,1},{1,0},{2,3},{3,2},{4,5},{5,4},{6,7},{7,6},{8,9},{9,8},{10,11... | collective-permute-start | bytes 1179656 | tf_op jit(solution)/shard_map/ppermute | solution.py:336
  54.0 24.5 %collective-permute-start.2 = (bf16[768,1024]{1,0:T(8,128)(2,1)S(1)}, bf16[768,1024]{1,0:T(8,128)(2,1)}, u32[]{:S(2)}, u32[]{:S(2)}) collective-permute-start(bf16[768,1024]{1,0:T(8,128)(2,1)S(1)} %copy-done.1), channel_id=1, source_target_pairs={{0,1},{1,0},{2,3},{3,2},{4,5},{5,4},{6,7},{7,6},{8,9},{9,8},{10,11... | collective-permute-start | bytes 4718600 | tf_op jit(solution)/shard_map/ppermute | solution.py:336
  54.5 36.1 %collective-permute-start.3 = (bf16[768,1024]{1,0:T(8,128)(2,1)S(1)}, bf16[768,1024]{1,0:T(8,128)(2,1)}, u32[]{:S(2)}, u32[]{:S(2)}) collective-permute-start(bf16[768,1024]{1,0:T(8,128)(2,1)S(1)} %add.75.refs_0_), channel_id=1, source_target_pairs={{0,2},{1,3},{2,0},{3,1},{4,6},{5,7},{6,4},{7,5},{8,10},{9,11},{10,... | collective-permute-start | bytes 4718600 | tf_op jit(solution)/shard_map/ppermute | solution.py:339
  54.9 61.0 %collective-permute-start.12 = (bf16[576,1024]{1,0:T(8,128)(2,1)}, bf16[576,1024]{1,0:T(8,128)(2,1)}, u32[]{:S(2)}, u32[]{:S(2)}) collective-permute-start(bf16[576,1024]{1,0:T(8,128)(2,1)} %join.1.refs_1_), channel_id=1, source_target_pairs={{0,2},{1,3},{2,0},{3,1},{4,6},{5,7},{6,4},{7,5},{8,10},{9,11},{10,... | collective-permute-start | bytes 3538952 | tf_op jit(solution)/shard_map/ppermute | solution.py:339
  58.0 1.3 copy-start.2
  99.2 0.6 copy-start.4
  99.8 0.7 copy-start.6
  115.9 0.9 copy-start.5
  115.9 6.6 %copy-start.7 = (bf16[192,1024]{1,0:T(8,128)(2,1)S(1)}, bf16[192,1024]{1,0:T(8,128)(2,1)}, u32[]{:S(2)}) copy-start(bf16[192,1024]{1,0:T(8,128)(2,1)} %copy-done.6) | copy-start | bytes 1179652
  115.9 9.6 %collective-permute-start.14 = (bf16[576,1024]{1,0:T(8,128)(2,1)}, bf16[576,1024]{1,0:T(8,128)(2,1)S(1)}, u32[]{:S(2)}, u32[]{:S(2)}) collective-permute-start(bf16[576,1024]{1,0:T(8,128)(2,1)} %hold.1.refs_1_), channel_id=1, source_target_pairs={{0,1},{1,0},{2,3},{3,2},{4,5},{5,4},{6,7},{7,6},{8,9},{9,8},{10,11... | collective-permute-start | bytes 3538952 | tf_op jit(solution)/shard_map/ppermute | solution.py:336
  116.7 8.8 %collective-permute-start.13 = (bf16[192,1024]{1,0:T(8,128)(2,1)}, bf16[192,1024]{1,0:T(8,128)(2,1)}, u32[]{:S(2)}, u32[]{:S(2)}) collective-permute-start(bf16[192,1024]{1,0:T(8,128)(2,1)} %collective-permute-done.1.refs_1_.refs_0_), channel_id=1, source_target_pairs={{0,1},{1,0},{2,3},{3,2},{4,5},{5,4},{6,7},{7,6},{8,9},{9,8},{10,11... | collective-permute-start | bytes 1179656 | tf_op jit(solution)/shard_map/ppermute | solution.py:336
  116.8 3.8 %collective-permute-start.17 = (f32[8,128]{1,0:T(8,128)S(1)}, f32[8,128]{1,0:T(8,128)S(1)}, u32[]{:S(2)}, u32[]{:S(2)}) collective-permute-start(f32[8,128]{1,0:T(8,128)S(1)} %copy-done.5), channel_id=1, source_target_pairs={{0,12},{4,0},{8,4},{12,8},{1,13},{5,1},{9,5},{13,9},{2,14},{6,2},{... | collective-permute-start | bytes 12296 | tf_op jit(solution)/shard_map/ppermute | solution.py:333
  116.9 3.8 %collective-permute-start.16 = (f32[8,128]{1,0:T(8,128)S(1)}, f32[8,128]{1,0:T(8,128)S(1)}, u32[]{:S(2)}, u32[]{:S(2)}) collective-permute-start(f32[8,128]{1,0:T(8,128)S(1)} %copy-done.5), channel_id=1, source_target_pairs={{0,8},{4,12},{8,0},{12,4},{1,9},{5,13},{9,1},{13,5},{2,10},{6,14},... | collective-permute-start | bytes 12296 | tf_op jit(solution)/shard_map/ppermute | solution.py:333
  118.3 4.3 %collective-permute-start.15 = (f32[8,128]{1,0:T(8,128)S(1)}, f32[8,128]{1,0:T(8,128)S(1)}, u32[]{:S(2)}, u32[]{:S(2)}) collective-permute-start(f32[8,128]{1,0:T(8,128)S(1)} %copy-done.5), channel_id=1, source_target_pairs={{0,4},{4,8},{8,12},{12,0},{1,5},{5,9},{9,13},{13,1},{2,6},{6,10},{... | collective-permute-start | bytes 12296 | tf_op jit(solution)/shard_map/ppermute | solution.py:333
  120.6 24.3 %collective-permute-start.9 = (bf16[192,1024]{1,0:T(8,128)(2,1)}, bf16[192,1024]{1,0:T(8,128)(2,1)S(1)}, u32[]{:S(2)}, u32[]{:S(2)}) collective-permute-start(bf16[192,1024]{1,0:T(8,128)(2,1)} %get-tuple-element.25), channel_id=1, source_target_pairs={{0,4},{4,8},{8,12},{12,0},{1,5},{5,9},{9,13},{13,1},{2,6},{6,10},{... | collective-permute-start | bytes 1179656 | tf_op jit(solution)/shard_map/ppermute | solution.py:333
  120.7 33.0 %collective-permute-start.10 = (bf16[192,1024]{1,0:T(8,128)(2,1)}, bf16[192,1024]{1,0:T(8,128)(2,1)S(1)}, u32[]{:S(2)}, u32[]{:S(2)}) collective-permute-start(bf16[192,1024]{1,0:T(8,128)(2,1)} %get-tuple-element.26), channel_id=1, source_target_pairs={{0,8},{4,12},{8,0},{12,4},{1,9},{5,13},{9,1},{13,5},{2,10},{6,14},... | collective-permute-start | bytes 1179656 | tf_op jit(solution)/shard_map/ppermute | solution.py:333
  122.5 35.1 %collective-permute-start.11 = (bf16[192,1024]{1,0:T(8,128)(2,1)S(1)}, bf16[192,1024]{1,0:T(8,128)(2,1)S(1)}, u32[]{:S(2)}, u32[]{:S(2)}) collective-permute-start(bf16[192,1024]{1,0:T(8,128)(2,1)S(1)} %copy-done.7), channel_id=1, source_target_pairs={{0,12},{4,0},{8,4},{12,8},{1,13},{5,1},{9,5},{13,9},{2,14},{6,2},{... | collective-permute-start | bytes 1179656 | tf_op jit(solution)/shard_map/ppermute | solution.py:333
